TPU v7x, 128 devices: a whole 4x4x4 slice. The times are simulated.
128 devices in a mesh: dom: 8 (over x_hi, y), fsdp: 16 (over x_lo, z, core).
Axes of the slice: x: 4 (x_hi: 2, x_lo: 2; x = x_hi * 2 + x_lo), y: 4, z: 4, core: 2. Of those that a mesh axis runs over, the one named last changes fastest.
Arguments:
- inputs: bfloat16 [8, 2048, 4096], P('dom', 'fsdp'), may hold values from -6 to 6
- cotangent: bfloat16 [8, 2048, 8192], P('dom', 'fsdp'), may hold values from -6 to 6
- shared_weight: bfloat16 [4096, 8192], P(None, 'fsdp'), may hold values from -0.09375 to 0.09375
- domain_weight: bfloat16 [8, 4096, 8192], P('dom', None, 'fsdp'), may hold values from 0.099609375 to 1.8984375
- row_counts: int32 [8], P('dom'), may hold values from 129 to 2048, as said below
Outputs:
- shared_grad: float32 [4096, 8192], P('dom', 'fsdp')
- domain_grad: bfloat16 [8, 4096, 8192], P('dom', None, 'fsdp')
- input_grad: bfloat16 [8, 2048, 4096], P('dom', 'fsdp')
Inputs may be any that keep to these rules, and one draw needn't show every extreme that they name: `row_counts`: rows of a domain at positions from its count on are padding. Some domain is full in every draw.
All inputs are finite; a program needn't handle non-finite values.
Results may differ from a plain program's by a relative error of at most 0.017.
Values may be sent and summed in bfloat16 or wider, within the bound.
No kernel may reach another device: no remote copies, remote signals or barrier semaphores. Data moves between devices by JAX's collectives and lax.ppermute only.
A program may use at most 128 MiB of HBM per device.

v0:
```python
import jax
import jax.numpy as jnp
from jax import lax
from jax.sharding import PartitionSpec as P


def body(inputs, cotangent, shared_weight, domain_weight, row_counts):
    effective = (shared_weight.astype(jnp.float32) * domain_weight[0].astype(jnp.float32)).astype(
        jnp.bfloat16
    )
    live_rows = row_counts[0]
    columns = lax.all_to_all(cotangent[0], "fsdp", split_axis=1, concat_axis=0, tiled=True)
    piece = lax.all_gather(inputs[0], "fsdp", axis=0, tiled=True)
    length = piece.shape[0]
    upstream = columns.astype(jnp.float32)
    preact = jnp.dot(piece, effective, preferred_element_type=jnp.float32)
    sigma = jax.nn.sigmoid(preact)
    position = lax.iota(jnp.int32, length)
    slope = upstream * sigma * (1.0 + preact * (1.0 - sigma))
    fold_grad_pre = jnp.where((position < live_rows)[:, None], slope, jnp.float32(0.0)).astype(
        jnp.bfloat16
    )
    weight_sum = lax.dot_general(
        piece, fold_grad_pre, (((0,), (0,)), ((), ())), preferred_element_type=jnp.float32
    )
    weight_sum, grad_pre = (weight_sum, fold_grad_pre)
    scaled = weight_sum * lax.rsqrt(live_rows.astype(jnp.float32))
    input_grad = lax.psum_scatter(
        lax.dot_general(
            grad_pre, effective, (((1,), (1,)), ((), ())), preferred_element_type=jnp.float32
        ).astype(jnp.bfloat16),
        "fsdp",
        scatter_dimension=0,
        tiled=True,
    )
    shared_grad = lax.psum_scatter(
        (scaled * domain_weight[0].astype(jnp.float32)).astype(jnp.bfloat16),
        "dom",
        scatter_dimension=0,
        tiled=True,
    ).astype(jnp.float32)
    domain_grad = (scaled * shared_weight.astype(jnp.float32)).astype(jnp.bfloat16)
    return (shared_grad, domain_grad[None], input_grad[None])


def solution(mesh):
    return jax.shard_map(
        body,
        mesh=mesh,
        in_specs=(
            P("dom", "fsdp", None),
            P("dom", "fsdp", None),
            P(None, "fsdp"),
            P("dom", None, "fsdp"),
            P("dom"),
        ),
        out_specs=(P("dom", "fsdp"), P("dom", None, "fsdp"), P("dom", "fsdp", None)),
        check_vma=False,
    )
```

profile of v0, /device:TPU:0, one launch (start us, length us, event | category | flops | bytes accessed | tf_op | source)
XLA Modules:
  0.0 354.0 jit_solution(5224221088672662130)
XLA Ops:
  7.2 0.0 all-gather.3.cloned.1.call-start
  7.2 0.7 all-gather.3.cloned.1.call-update
  7.9 4.1 %copy.13 = bf16[1,128,8192]{1,2,0:T(8,128)(2,1)} copy(bf16[1,128,8192]{2,1,0:T(8,128)(2,1)} %param.6) | data formatting | bytes 4194304 | tf_op args[1]
  12.0 6.4 %all-to-all-start = ((bf16[128,16,512]{0,2,1:T(8,128)(2,1)}), bf16[128,16,512]{0,2,1:T(8,128)(2,1)S(1)}, u32[]{:S(2)}, u32[]{:S(2)}) async-start(bf16[128,16,512]{0,2,1:T(8,128)(2,1)} %bitcast.1), calls=%async_computation | async-start | bytes 4194304 | tf_op jit(solution)/shard_map/all_to_all | solution.py:12
  18.4 0.0 reduce-scatter.3.cloned.1.call-start
  19.1 6.4 %copy.15 = bf16[4096,512]{0,1:T(8,128)(2,1)} copy(bf16[4096,512]{1,0:T(8,128)(2,1)} %param.7) | data formatting | bytes 8388608 | tf_op args[2]
  25.5 6.5 %copy.16 = bf16[1,4096,512]{1,2,0:T(8,128)(2,1)} copy(bf16[1,4096,512]{2,1,0:T(8,128)(2,1)} %param.8) | data formatting | bytes 8388608 | tf_op args[3]
  32.0 92.5 %all-gather.3.cloned.1.call-done = bf16[1,2048,4096]{2,1,0:T(8,128)(2,1)} async-done(((bf16[1,128,4096]{2,1,0:T(8,128)(2,1)}), bf16[1,2048,4096]{2,1,0:T(8,128)(2,1)}) %all-gather.3.cloned.1.call-update) | async-done | bytes 16777232 | tf_op jit(solution)/shard_map/all_gather | solution.py:13
  124.5 16.3 %fusion.2 = f32[512,2048]{1,0:T(8,128)} fusion(bf16[1,2048,4096]{2,1,0:T(8,128)(2,1)} %all-gather.3.cloned.1.call-done, bf16[4096,512]{0,1:T(8,128)(2,1)} %copy.15, bf16[1,4096,512]{1,2,0:T(8,128)(2,1)} %copy.16), kind=kOutput, calls=%fused_computation.2 | convolution fusion | flops 8598323200 | bytes 29360128 | tf_op jit(solution)/shard_map/dot_general | solution.py:16
  140.9 0.0 all-to-all-done
  140.9 20.7 %fusion.7 = (bf16[1,4096,512]{1,2,0:T(8,128)(2,1)}, bf16[4096,512]{0,1:T(8,128)(2,1)}) fusion(bf16[4096,512]{0,1:T(8,128)(2,1)} %copy.15, f32[]{:T(128)S(6)} %rsqrt.3, bf16[1,4096,512]{1,2,0:T(8,128)(2,1)} %copy.16, bf16[1,2048,4096]{2,1,0:T(8,128)(2,1)} %all-gather.3.cloned.1.call-done, f32[512,2048]{1,0:T(8,128)} %fusion.2, ...), kind=kOutput, calls=%fused_computation.11 | convolution fusion | flops 8616148992 | bytes 39847940 | tf_op jit(solution)/shard_map/dot_general | solution.py:23
  161.6 0.0 reduce-scatter.3.cloned.1.call-update
  161.6 0.2 reduce-scatter.5.cloned.1.call-start
  161.9 18.8 %convolution_convert_fusion = bf16[2048,4096]{1,0:T(8,128)(2,1)} fusion(f32[512,2048]{1,0:T(8,128)} %fusion.2, pred[2048]{0:T(1024)(128)(4,1)S(1)} %iota_compare_fusion, bf16[4096,512]{0,1:T(8,128)(2,1)} %copy.15, bf16[1,4096,512]{1,2,0:T(8,128)(2,1)} %copy.16, bf16[128,16,512]{0,2,1:T(8,128)(2,1)S(1)} %all-to-all-done), kind=kOutput, calls=%fused_computation.4 | convolution fusion | flops 8618246144 | bytes 31459328 | tf_op jit(solution)/shard_map/dot_general | solution.py:29
  180.7 0.0 reduce-scatter.5.cloned.1.call-update
  180.7 6.4 %copy.18 = bf16[1,4096,512]{2,1,0:T(8,128)(2,1)} copy(bf16[1,4096,512]{1,2,0:T(8,128)(2,1)} %get-tuple-element.9) | data formatting | bytes 8388608
  187.1 59.9 %reduce-scatter.3.cloned.1.call-done = bf16[512,512]{0,1:T(8,128)(2,1)} async-done(((bf16[4096,512]{0,1:T(8,128)(2,1)}), bf16[512,512]{0,1:T(8,128)(2,1)}) %reduce-scatter.3.cloned.1.call-update) | async-done | bytes 524304 | tf_op jit(solution)/shard_map/reduce_scatter | solution.py:36
  247.1 2.2 copy.17
  249.3 98.2 %reduce-scatter.5.cloned.1.call-done = bf16[128,4096]{1,0:T(8,128)(2,1)} async-done(((bf16[2048,4096]{1,0:T(8,128)(2,1)}), bf16[128,4096]{1,0:T(8,128)(2,1)}) %reduce-scatter.5.cloned.1.call-update) | async-done | bytes 1048592 | tf_op jit(solution)/shard_map/reduce_scatter | solution.py:28
  (1 shorter events, 0.0 us)
Async XLA Ops:
  7.2 117.4 %all-gather.3.cloned.1.call-start = ((), (), s32[]{:S(2)}) async-start(), calls=%async_computation.5 | async-start | bytes 17825792 | tf_op jit(solution)/shard_map/all_gather | solution.py:13
  12.0 128.9 %all-to-all-start = ((bf16[128,16,512]{0,2,1:T(8,128)(2,1)}), bf16[128,16,512]{0,2,1:T(8,128)(2,1)S(1)}, u32[]{:S(2)}, u32[]{:S(2)}) async-start(bf16[128,16,512]{0,2,1:T(8,128)(2,1)} %bitcast.1), calls=%async_computation | async-start | bytes 4194304 | tf_op jit(solution)/shard_map/all_to_all | solution.py:12
  18.4 228.7 %reduce-scatter.3.cloned.1.call-start = ((), (), s32[]{:S(2)}) async-start(), calls=%async_computation.3 | async-start | bytes 4718592 | tf_op jit(solution)/shard_map/reduce_scatter | solution.py:36
  161.6 185.9 %reduce-scatter.5.cloned.1.call-start = ((), (), s32[]{:S(2)}) async-start(), calls=%async_computation.4 | async-start | bytes 17825792 | tf_op jit(solution)/shard_map/reduce_scatter | solution.py:28
Sparse Core Ops, SparseCore 0:
  9.7 114.7 all-gather.2
  161.7 85.2 reduce-scatter.2
  250.2 97.2 reduce-scatter.4
where the time goes:
time: 355 us; the launch traced here: 354 us
  waiting for transfers between devices  251 us (71%)
  matrix products  55.9 us (16%)
  local copies, waits for them, and re-layouts  25.6 us (7%)
  between operations  14.4 us (4%)
  starting transfers between devices  6.73 us (2%)
    reduce_scatter x1, waiting for transfers between devices, body(): lax.psum_scatter(lax.dot_general(grad_pre, effective, (((1,), (1,)), ((),...  98.2 us
    all_gather x1, waiting for transfers between devices, body(): piece = lax.all_gather(inputs[0], 'fsdp', axis=0, tiled=True)  92.5 us
    reduce_scatter x1, waiting for transfers between devices, body(): lax.psum_scatter((scaled * domain_weight[0].astype(jnp.float32)).astype(j...  59.9 us
    unnamed x5, local copies, waits for them, and re-layouts  25.6 us
    dot_general x1, matrix products, body(): lax.dot_general(piece, fold_grad_pre, (((0,), (0,)), ((), ())), preferred...  20.7 us
    dot_general x1, matrix products, body(): lax.dot_general(grad_pre, effective, (((1,), (1,)), ((), ())), preferred_...  18.8 us
    dot_general x1, matrix products, body(): preact = jnp.dot(piece, effective, preferred_element_type=jnp.float32)  16.3 us
  transfers between devices with their start and end apart: 4, of which 3 were waited for; matrix products, arithmetic and copies ran while one was open for 17% of the time, Pallas kernels for 0%

commit v1 on v0

v1 whole, which is shorter than its diff:
```python
import functools

import jax
import jax.numpy as jnp
from jax import lax
from jax.experimental import pallas as pl
from jax.experimental.pallas import tpu as pltpu
from jax.sharding import PartitionSpec as P

BF = jnp.bfloat16
F32 = jnp.float32
NX, NZ, NC = 2, 4, 2
NXH, NY = 2, 4
ROWS = 128
HALF = ROWS // 2
D = 4096
UNITS = 512
MIB = 1 << 20
VMEM_LIMIT = 60 * MIB
SMALL = pl.CostEstimate(flops=1 << 20, bytes_accessed=1 << 16, transcendentals=0)


def fsdp_pairs(dx, dz, dc):
    pairs = []
    for x in range(NX):
        for z in range(NZ):
            for c in range(NC):
                to = (((x + dx) % NX) * NZ + (z + dz) % NZ) * NC + (c + dc) % NC
                pairs.append(((x * NZ + z) * NC + c, to))
    return pairs


def dom_pairs(dh, dy):
    return [
        (h * NY + y, ((h + dh) % NXH) * NY + (y + dy) % NY) for h in range(NXH) for y in range(NY)
    ]


def send(value, dx=0, dz=0, dc=0):
    return lax.ppermute(value, "fsdp", fsdp_pairs(dx, dz, dc))


def send_dom(value, dh=0, dy=0):
    return lax.ppermute(value, "dom", dom_pairs(dh, dy))


def tiled_dot(lhs, rhs, contract):
    return lax.dot_general(lhs, rhs, (contract, ((), ())), preferred_element_type=F32)


CHUNK = 2 * UNITS


def split_kernel(up_ref, out_ref, held, in_sem, out_sem):
    n = NX * NZ
    loads, stores = [], []
    for k in range(n):
        cols = pl.ds(k * 2 * UNITS, 2 * UNITS)
        loads.append(pltpu.make_async_copy(up_ref.at[:, cols], held.at[k], in_sem.at[k]))
        stores.append(pltpu.make_async_copy(held.at[k], out_ref.at[k], out_sem.at[k]))
    for copy in loads:
        copy.start()
    for load, store in zip(loads, stores):
        load.wait()
        store.start()
    for copy in stores:
        copy.wait()


def split_cotangent(up):
    n = NX * NZ
    any_spec = pl.BlockSpec(memory_space=pl.ANY)
    return pl.pallas_call(
        split_kernel,
        out_shape=jax.ShapeDtypeStruct((n, ROWS, 2 * UNITS), BF),
        in_specs=[any_spec],
        out_specs=any_spec,
        scratch_shapes=[
            pltpu.VMEM((n, ROWS, 2 * UNITS), BF),
            pltpu.SemaphoreType.DMA((n,)),
            pltpu.SemaphoreType.DMA((n,)),
        ],
        compiler_params=pltpu.CompilerParams(vmem_limit_bytes=VMEM_LIMIT),
        cost_estimate=SMALL,
    )(up)


def chip_of(meta, dx, dz):
    return lax.rem(meta[2] + dx, NX) * NZ + lax.rem(meta[3] + dz + NZ, NZ)


def block_kernel(pieces, out_map, meta, *refs):
    n, n_out = len(pieces), 1 + max(k for k, _ in out_map)
    x_refs, cot_ref, eff_refs = refs[:n], refs[n], refs[n + 1 : n + 5]
    outs = refs[n + 5 : n + 5 + n_out]
    grad_ref, both_ref = refs[n + 5 + n_out : n + 7 + n_out]
    xs, eff, cot, grad, dx, x_sem, e_sem, c_sem, o_sem, g_sem = refs[n + 7 + n_out :]
    live, core = meta[0], meta[1]
    copies, c_copies = [], []
    begin = 0
    for i, (rows, row, _) in enumerate(pieces):
        place = pl.ds(begin, rows)
        copies.append(pltpu.make_async_copy(x_refs[i], xs.at[place], x_sem.at[i]))
        c_copies.append(
            pltpu.make_async_copy(
                cot_ref.at[chip_of(meta, *pieces[i][2]), pl.ds(row, rows)], cot.at[place], c_sem.at[i]
            )
        )
        begin += rows
    e_copies = [
        pltpu.make_async_copy(
            eff_refs[2 * u + h], eff.at[u, pl.ds(h * D // 2, D // 2)], e_sem.at[u, h]
        )
        for u in range(2)
        for h in range(2)
    ]
    for copy in copies + e_copies[:2] + c_copies:
        copy.start()
    for copy in copies:
        copy.wait()
    for u in range(2):
        for copy in e_copies[2 * u : 2 * u + 2]:
            copy.wait()
        if u == 0:
            for copy in e_copies[2:]:
                copy.start()
            for copy in c_copies:
                copy.wait()
        col = pl.multiple_of((core if u == 0 else 1 - core) * UNITS, UNITS)

        @pl.loop(0, UNITS // 256)
        def _(k):
            at = pl.multiple_of(k * 256, 256)
            pre = tiled_dot(xs[...], eff[u, :, pl.ds(at, 256)], ((1,), (0,)))
            begin = 0
            for rows, row, to in pieces:
                v = pre[begin : begin + rows]
                up = cot[pl.ds(begin, rows), pl.ds(pl.multiple_of(col + at, 256), 256)].astype(F32)
                s = jax.nn.sigmoid(v)
                slope = up * s * (1.0 + v * (1.0 - s))
                first = (chip_of(meta, *to) * NC + core) * ROWS + row
                position = first + lax.broadcasted_iota(jnp.int32, (rows, 256), 0)
                slope = jnp.where(position < live, slope, 0.0)
                grad[u, pl.ds(begin, rows), pl.ds(at, 256)] = slope.astype(BF)
                begin += rows

    r_copy = pltpu.make_async_copy(xs, both_ref.at[:, pl.ds(0, D)], g_sem.at[1])
    r_copy.start()
    g_copies = [
        pltpu.make_async_copy(grad.at[0], grad_ref, g_sem.at[0]),
        pltpu.make_async_copy(grad.at[1], both_ref.at[:, pl.ds(D, UNITS)], g_sem.at[2]),
    ]
    for copy in g_copies:
        copy.start()

    @pl.loop(0, D // 512)
    def _(k):
        at = pl.multiple_of(k * 512, 512)
        part = tiled_dot(grad[0], eff[0, pl.ds(at, 512), :], ((1,), (1,)))
        part += tiled_dot(grad[1], eff[1, pl.ds(at, 512), :], ((1,), (1,)))
        dx[:, pl.ds(at, 512)] = part.astype(BF)
        for i, (k, row) in enumerate(out_map):
            pltpu.make_async_copy(
                dx.at[pl.ds(i * HALF, HALF), pl.ds(at, 512)],
                outs[k].at[pl.ds(row, HALF), pl.ds(at, 512)],
                o_sem.at[i],
            ).start()

    for i, (k, row) in enumerate(out_map):
        pltpu.make_async_copy(
            dx.at[pl.ds(i * HALF, HALF)], outs[k].at[pl.ds(row, HALF)], o_sem.at[i]
        ).wait()
    for copy in g_copies + [r_copy]:
        copy.wait()


def block_pass(blocks, out_map, out_rows, eff, cot, meta):
    xs, rows_at, chips = zip(*blocks)
    pieces = tuple((x.shape[0], row, to) for x, row, to in zip(xs, rows_at, chips))
    n = len(blocks)
    total = sum(piece[0] for piece in pieces)
    any_spec = pl.BlockSpec(memory_space=pl.ANY)
    outs = pl.pallas_call(
        functools.partial(block_kernel, pieces, tuple(out_map)),
        out_shape=[jax.ShapeDtypeStruct((r, D), BF) for r in out_rows]
        + [
            jax.ShapeDtypeStruct((total, UNITS), BF),
            jax.ShapeDtypeStruct((total, D + UNITS), BF),
        ],
        in_specs=[pl.BlockSpec(memory_space=pltpu.SMEM)] + [any_spec] * (n + 5),
        out_specs=[any_spec] * (len(out_rows) + 2),
        scratch_shapes=[
            pltpu.VMEM((total, D), BF),
            pltpu.VMEM((2, D, UNITS), BF),
            pltpu.VMEM((total, CHUNK), BF),
            pltpu.VMEM((2, total, UNITS), BF),
            pltpu.VMEM((total, D), BF),
            pltpu.SemaphoreType.DMA((n,)),
            pltpu.SemaphoreType.DMA((2, 2)),
            pltpu.SemaphoreType.DMA((n,)),
            pltpu.SemaphoreType.DMA((len(out_map),)),
            pltpu.SemaphoreType.DMA((3,)),
        ],
        compiler_params=pltpu.CompilerParams(vmem_limit_bytes=VMEM_LIMIT),
        cost_estimate=SMALL,
    )(meta, *xs, cot, *eff)
    return outs[:-2], outs[-2], outs[-1]


def weight_kernel(n, dh, meta, scale, *refs):
    mine, grads, others = refs[:n], refs[n : 2 * n], refs[2 * n : 3 * n]
    shared_ref, domain_ref, _ = refs[3 * n : 3 * n + 3]
    terms, dgrad_ref = refs[3 * n + 3 : 3 * n + 7], refs[3 * n + 7]
    xs, gs, shared, domain, term, dgrad, x_sem, g_sem, w_sem, o_sem = refs[3 * n + 8 :]
    h = lax.rem(meta[4] + dh, NXH)
    order = [h * NY + lax.rem(meta[5] + dy, NY) for dy in (2, 1, 3, 0)]
    g_copies, loads = [], [[] for _ in range(4)]
    begin = 0
    for i in range(2 * n):
        x_ref = (mine + others)[i]
        rows = x_ref.shape[0]
        g_ref = grads[i] if i < n else x_ref.at[:, pl.ds(D, UNITS)]
        place = pl.ds(begin, rows)
        g_copies.append(pltpu.make_async_copy(g_ref, gs.at[place], g_sem.at[i]))
        for k in range(4):
            cols = pl.ds(pl.multiple_of(order[k] * 512, 512), 512)
            loads[k].append(
                pltpu.make_async_copy(x_ref.at[:, cols], xs.at[k, place], x_sem.at[k, i])
            )
        begin += rows
    for k in range(4):
        rows = pl.ds(pl.multiple_of(order[k] * 512, 512), 512)
        loads[k] += [
            pltpu.make_async_copy(shared_ref.at[rows], shared.at[k], w_sem.at[0, k]),
            pltpu.make_async_copy(domain_ref.at[rows], domain.at[k], w_sem.at[1, k]),
        ]
    for copy in g_copies + loads[0] + loads[1]:
        copy.start()
    for copy in g_copies:
        copy.wait()
    stores = []
    for k in range(4):
        for copy in loads[k]:
            copy.wait()
        if k < 2:
            for copy in loads[k + 2]:
                copy.start()
        whole = tiled_dot(xs[k], gs[...], ((0,), (0,))) * scale[0]
        dgrad[k] = (whole * shared[k].astype(F32)).astype(BF)
        term[k] = (whole * domain[k].astype(F32)).astype(BF)
        rows = pl.ds(pl.multiple_of(order[k] * 512, 512), 512)
        stores.append(pltpu.make_async_copy(term.at[k], terms[k], o_sem.at[0, k]))
        stores.append(pltpu.make_async_copy(dgrad.at[k], dgrad_ref.at[rows], o_sem.at[1, k]))
        for copy in stores[-2:]:
            copy.start()
    for copy in stores:
        copy.wait()


def weight_pass(mine, grads, others, shared_weight, domain_weight, before, dh, meta, scale):
    n = len(mine)
    total = 2 * sum(x.shape[0] for x in mine)
    any_spec = pl.BlockSpec(memory_space=pl.ANY)
    return pl.pallas_call(
        functools.partial(weight_kernel, n, dh),
        in_specs=[pl.BlockSpec(memory_space=pltpu.SMEM)] * 2 + [any_spec] * (3 * n + 3),
        out_specs=[any_spec] * 5,
        scratch_shapes=[pltpu.VMEM((4, total, 512), BF), pltpu.VMEM((total, UNITS), BF)]
        + [pltpu.VMEM((4, 512, UNITS), BF)] * 4
        + [
            pltpu.SemaphoreType.DMA((4, 2 * n)),
            pltpu.SemaphoreType.DMA((2 * n,)),
            pltpu.SemaphoreType.DMA((2, 4)),
            pltpu.SemaphoreType.DMA((2, 4)),
        ],
        out_shape=[jax.ShapeDtypeStruct((512, UNITS), BF)] * 4
        + [jax.ShapeDtypeStruct((D, UNITS), BF)],
        input_output_aliases={} if before is None else {2 + 3 * n + 2: 4},
        compiler_params=pltpu.CompilerParams(vmem_limit_bytes=VMEM_LIMIT),
        cost_estimate=SMALL,
    )(
        meta, scale, *mine, *grads, *others, shared_weight, domain_weight,
        scale if before is None else before,
    )


def add(*terms):
    return sum(t.astype(F32) for t in terms).astype(BF)


def split_last(values):
    return values[:-1], values[-1]


def together(*values):
    return lax.optimization_barrier(values)


def after(value, *others):
    return lax.optimization_barrier((value,) + others)[0]


def body(inputs, cotangent, shared_weight, domain_weight, row_counts):
    rows_in = inputs[0]
    dweight = domain_weight[0]
    live = row_counts[0]
    me = lax.axis_index("fsdp")
    x_at, z_at, core = me // (NZ * NC), (me // NC) % NZ, me % NC
    dom = lax.axis_index("dom")
    h_at, y_at = dom // NY, dom % NY

    meta = jnp.stack([live, core, x_at, z_at, h_at, y_at]).astype(jnp.int32)
    m1, p1, q0 = send(rows_in, dz=1), send(rows_in, dz=-1), send(rows_in, dx=1)
    chunks = split_cotangent(cotangent[0])
    cot = lax.all_to_all(
        chunks,
        "fsdp",
        split_axis=0,
        concat_axis=0,
        tiled=True,
        axis_index_groups=[[i * NC + c for i in range(NX * NZ)] for c in range(NC)],
    )
    weight = after(shared_weight, chunks)
    eff = [
        (weight[h : h + D // 2].astype(F32) * dweight[h : h + D // 2].astype(F32)).astype(BF)
        for h in (0, D // 2)
    ]
    eff += [send(part, dc=1) for part in eff]
    m1, p1, q0 = together(m1, p1, q0)
    qm, o2, qp = send(q0, dz=1), send(p1, dz=-1), send(p1, dx=1)

    common = (eff, cot, meta)
    (d_own, d_m1, d_p1, d_q0), g_near, x_near = block_pass(
        [
            (rows_in, 0, (0, 0)),
            (m1, 0, (0, -1)),
            (p1, 0, (0, 1)),
            (q0, 0, (1, 0)),
        ],
        [(k, row) for k in range(4) for row in (0, HALF)],
        [ROWS] * 4,
        *common,
    )
    qm, o2, qp, x_near = together(qm, o2, qp, x_near)
    q2a, q2b = send(qm[:HALF], dz=1), send(qp[HALF:], dz=-1)
    other_near = send(x_near, dc=1)
    (to_across, d_o2a, d_o2b, d_qma, d_qpb), g_mid, x_mid = block_pass(
        [(qp, 0, (1, 1)), (o2, 0, (0, 2)), (qm, 0, (1, -1))],
        [(0, 0), (4, 0), (1, 0), (2, 0), (3, 0), (0, HALF)],
        [ROWS, HALF, HALF, HALF, HALF],
        *common,
    )
    q2a, q2b, other_near, to_across, d_o2a, d_o2b, x_mid = together(
        q2a, q2b, other_near, to_across, d_o2a, d_o2b, x_mid
    )
    from_across = send(to_across, dx=1)
    o2_right = send(d_o2a, dz=-1)
    o2_left = send(d_o2b, dz=1)
    other_mid = send(x_mid, dc=1)
    (d_q2a, d_q2b), g_far, x_far = block_pass(
        [(q2a, 0, (1, 2)), (q2b, HALF, (1, 2))], [(0, 0), (1, 0)], [HALF, HALF], *common
    )
    o2_right, o2_left, other_mid, d_q2a, d_q2b, x_far = together(
        o2_right, o2_left, other_mid, d_q2a, d_q2b, x_far
    )
    q2_right = send(d_q2a, dz=-1)
    q2_left = send(d_q2b, dz=1)
    other_far = send(x_far, dc=1)

    mine, grads = [x_near, x_mid, x_far], [g_near, g_mid, g_far]
    others = [other_near, other_mid, other_far]
    scale = lax.rsqrt(live.astype(F32)).reshape(1)
    (far0, right0, left0, mine0), domain_grad = split_last(
        weight_pass(mine, grads, others, shared_weight, dweight, None, 1, meta, scale)
    )
    q2_right, q2_left, far0, left0, right0, domain_grad = together(
        q2_right, q2_left, far0, left0, right0, domain_grad
    )
    far0, left0 = send_dom(far0, dy=1), send_dom(left0, dy=-1)
    back_a = send(add(d_qma, q2_right), dz=-1)
    back_b = send(add(d_qpb, q2_left), dz=1)
    (far1, right1, left1, mine1), domain_grad = split_last(
        weight_pass(mine, grads, others, shared_weight, dweight, domain_grad, 0, meta, scale)
    )
    from_across, far0, left0, back_a, back_b, far1, right1, left1 = together(
        from_across, far0, left0, back_a, back_b, far1, right1, left1
    )
    right0 = send_dom(add(right0, far0), dy=1)
    far1 = send_dom(far1, dy=-1)
    end_c = send(add(d_q0, jnp.concatenate([back_a, back_b])), dx=1)
    end_a = send(add(d_m1, jnp.concatenate([o2_right, from_across[HALF:]])), dz=-1)
    end_b = send(add(d_p1, jnp.concatenate([from_across[:HALF], o2_left])), dz=1)
    right0, far1, right1 = together(right0, far1, right1)
    right1 = send_dom(right1, dy=1)
    left1 = send_dom(add(left1, far1), dy=-1)
    given = send_dom(add(mine0, left0, right0), dh=1)
    input_grad = add(d_own, end_a, end_b, end_c)
    mine1 = after(mine1, input_grad)
    shared_grad = sum(t.astype(F32) for t in (mine1, left1, right1, given))
    return (shared_grad, domain_grad[None], input_grad[None])


def solution(mesh):
    return jax.shard_map(
        body,
        mesh=mesh,
        in_specs=(
            P("dom", "fsdp", None),
            P("dom", "fsdp", None),
            P(None, "fsdp"),
            P("dom", None, "fsdp"),
            P("dom"),
        ),
        out_specs=(P("dom", "fsdp"), P("dom", None, "fsdp"), P("dom", "fsdp", None)),
        check_vma=False,
    )
```

time: 355 us -> 194 us (0.55)
  waiting for transfers between devices: 251 us -> 67.7 us
  Pallas kernels: 0 us -> 65.7 us
  matrix products: 55.9 us -> 0 us
  starting transfers between devices: 6.73 us -> 39.4 us
  local copies, waits for them, and re-layouts: 25.6 us -> 6 us
  between operations: 14.4 us -> 1.66 us
  other arithmetic: 0.01 us -> 12.6 us
    reduce_scatter x2 -> x0, waiting for transfers between devices: 158 us -> none  [the longest x1 98.2 us: body(): lax.psum_scatter(lax.dot_general(grad_pre, effective, (((1,), (1,)), ((),...]
    all_gather x1 -> x0, waiting for transfers between devices: 92.5 us -> none  [body(): piece = lax.all_gather(inputs[0], 'fsdp', axis=0, tiled=True)]
    ppermute x0 -> x30, waiting for transfers between devices: none -> 67.2 us  [the longest x23 53.9 us: send(): return lax.ppermute(value, 'fsdp', fsdp_pairs(dx, dz, dc))]
    pallas_call x0 -> x6, Pallas kernels: none -> 65.7 us  [the longest x3 41.8 us: block_pass(): pl.pallas_call(functools.partial(block_kernel, pieces, tuple(out_map)), o...]
    dot_general x3 -> x0, matrix products: 55.9 us -> none  [the longest x1 20.7 us: body(): lax.dot_general(piece, fold_grad_pre, (((0,), (0,)), ((), ())), preferred...]
    ppermute x0 -> x30, starting transfers between devices: none -> 34.8 us  [the longest x23 22.6 us: send(): return lax.ppermute(value, 'fsdp', fsdp_pairs(dx, dz, dc))]
    unnamed x5 -> x38, local copies, waits for them, and re-layouts: 25.6 us -> 2.76 us
    convert_element_type x0 -> x10, other arithmetic: none -> 11.4 us  [the longest x9 6.39 us: add(): return sum((t.astype(F32) for t in terms)).astype(BF)]
  transfers between devices with their start and end apart: 4 -> 31, of which waited for: 3 -> 15; matrix products, arithmetic and copies ran while one was open for 17% -> 7% of each run, Pallas kernels for 0% -> 34%
where the time goes in v1:
time: 194 us; the launch traced here: 193 us
  waiting for transfers between devices  67.7 us (35%)
  Pallas kernels  65.7 us (34%)
  starting transfers between devices  39.4 us (20%)
  other arithmetic  12.6 us (6%)
  local copies, waits for them, and re-layouts  6 us (3%)
    ppermute x23, waiting for transfers between devices, send(): return lax.ppermute(value, 'fsdp', fsdp_pairs(dx, dz, dc))  53.9 us
    pallas_call x3, Pallas kernels, block_pass(): pl.pallas_call(functools.partial(block_kernel, pieces, tuple(out_map)), o...  41.8 us
    ppermute x23, starting transfers between devices, send(): return lax.ppermute(value, 'fsdp', fsdp_pairs(dx, dz, dc))  22.6 us
    pallas_call x2, Pallas kernels, weight_pass(): pl.pallas_call(functools.partial(weight_kernel, n, dh), in_specs=[pl.Bloc...  21.5 us
    ppermute x7, waiting for transfers between devices, send_dom(): return lax.ppermute(value, 'dom', dom_pairs(dh, dy))  13.2 us
    ppermute x7, starting transfers between devices, send_dom(): return lax.ppermute(value, 'dom', dom_pairs(dh, dy))  12.3 us
    convert_element_type x9, other arithmetic, add(): return sum((t.astype(F32) for t in terms)).astype(BF)  6.39 us
    convert_element_type x1, other arithmetic, body(): (weight[h:h + D // 2].astype(F32) * dweight[h:h + D // 2].astype(F32)).as...  5 us
  transfers between devices with their start and end apart: 31, of which 15 were waited for; matrix products, arithmetic and copies ran while one was open for 7% of the time, Pallas kernels for 34%

profile of v1, /device:TPU:0, one launch (start us, length us, event | category | flops | bytes accessed | tf_op | source)
XLA Modules:
  0.0 193.1 jit_solution(11338957976767752718)
XLA Ops:
  0.6 1.7 collective-permute-start.2
  2.3 4.0 %collective-permute-start.1 = (bf16[128,4096]{1,0:T(8,128)(2,1)}, bf16[128,4096]{1,0:T(8,128)(2,1)S(1)}, u32[]{:S(2)}, u32[]{:S(2)}) collective-permute-start(bf16[128,4096]{1,0:T(8,128)(2,1)} %bitcast.21), channel_id=1, source_target_pairs={{0,6},{1,7},{2,0},{3,1},{4,2},{5,3},{6,4},{7,5},{8,14},{9,15},{10,... | collective-permute-start | bytes 3145736 | tf_op jit(solution)/shard_map/ppermute | solution.py:40
  6.3 2.4 %shard_map.76 = bf16[8,128,1024]{2,1,0:T(8,128)(2,1)} custom-call(bf16[128,8192]{1,0:T(8,128)(2,1)} %bitcast.19), custom_call_target="tpu_custom_call" | custom-call | flops 1048576 | bytes 65536 | tf_op jit(solution)/shard_map/pallas_call | solution.py:73
  8.7 5.0 %fusion = (bf16[2048,512]{1,0:T(8,128)(2,1)S(1)}, bf16[2048,512]{1,0:T(8,128)(2,1)}) fusion(bf16[1,4096,512]{2,1,0:T(8,128)(2,1)} %param.8, bf16[4096,512]{1,0:T(8,128)(2,1)} %refs_9_.3), kind=kLoop, calls=%fused_computation.1 | loop fusion | flops 8388608 | bytes 12582912 | tf_op jit(solution)/shard_map/convert_element_type | solution.py:325
  13.7 0.5 collective-permute-start.6
  14.2 0.8 copy-done
  15.0 4.5 %all-to-all-start = ((bf16[8,128,1024]{2,1,0:T(8,128)(2,1)}), bf16[8,128,1024]{2,1,0:T(8,128)(2,1)}, u32[]{:S(2)}, u32[]{:S(2)}) async-start(bf16[8,128,1024]{2,1,0:T(8,128)(2,1)} %shard_map.76), calls=%async_computation | async-start | bytes 4194304 | tf_op jit(solution)/shard_map/all_to_all | solution.py:315
  19.5 7.5 %collective-permute-done.2.refs_3_ = bf16[128,4096]{1,0:T(8,128)(2,1)} collective-permute-done((bf16[128,4096]{1,0:T(8,128)(2,1)}, bf16[128,4096]{1,0:T(8,128)(2,1)}, u32[]{:S(2)}, u32[]{:S(2)}) %collective-permute-start.2) | collective-permute-done | bytes 1048608 | tf_op jit(solution)/shard_map/ppermute | solution.py:40
  27.1 14.4 %collective-permute-done.1.refs_2_ = bf16[128,4096]{1,0:T(8,128)(2,1)S(1)} collective-permute-done((bf16[128,4096]{1,0:T(8,128)(2,1)}, bf16[128,4096]{1,0:T(8,128)(2,1)S(1)}, u32[]{:S(2)}, u32[]{:S(2)}) %collective-permute-start.1) | collective-permute-done | bytes 1048608 | tf_op jit(solution)/shard_map/ppermute | solution.py:40
  41.5 1.0 copy-done.5
  42.4 8.4 %collective-permute-done.refs_1_ = bf16[128,4096]{1,0:T(8,128)(2,1)} collective-permute-done((bf16[128,4096]{1,0:T(8,128)(2,1)}, bf16[128,4096]{1,0:T(8,128)(2,1)}, u32[]{:S(2)}, u32[]{:S(2)}) %collective-permute-start) | collective-permute-done | bytes 1048608 | tf_op jit(solution)/shard_map/ppermute | solution.py:40
  50.8 0.5 collective-permute-start.5
  51.3 3.2 %collective-permute-start.4 = (bf16[128,4096]{1,0:T(8,128)(2,1)}, bf16[128,4096]{1,0:T(8,128)(2,1)}, u32[]{:S(2)}, u32[]{:S(2)}) collective-permute-start(bf16[128,4096]{1,0:T(8,128)(2,1)} %copy-done.5), channel_id=1, source_target_pairs={{0,6},{1,7},{2,0},{3,1},{4,2},{5,3},{6,4},{7,5},{8,14},{9,15},{10,... | collective-permute-start | bytes 3145736 | tf_op jit(solution)/shard_map/ppermute | solution.py:40
  55.2 0.6 stack.23.meta
  55.9 0.6 all-to-all-done.refs_4_.refs_3_.refs_2_
  56.4 16.7 %shard_map.77 = (bf16[128,4096]{1,0:T(8,128)(2,1)}, bf16[128,4096]{1,0:T(8,128)(2,1)}, bf16[128,4096]{1,0:T(8,128)(2,1)}, bf16[128,4096]{1,0:T(8,128)(2,1)}, bf1...) custom-call(s32[6]{0:T(128)} %stack.23.meta, bf16[128,4096]{1,0:T(8,128)(2,1)} %bitcast.23, ...), custom_call_target="tpu_custom_call" | custom-call | flops 1048576 | bytes 65536 | tf_op jit(solution)/shard_map/pallas_call | solution.py:183
  73.1 3.9 %collective-permute-done.3.refs_2_ = bf16[128,4096]{1,0:T(8,128)(2,1)S(1)} collective-permute-done((bf16[128,4096]{1,0:T(8,128)(2,1)}, bf16[128,4096]{1,0:T(8,128)(2,1)S(1)}, u32[]{:S(2)}, u32[]{:S(2)}) %collective-permute-start.3) | collective-permute-done | bytes 1048608 | tf_op jit(solution)/shard_map/ppermute | solution.py:40
  77.0 0.1 collective-permute-start.10
  77.2 1.3 slice.31
  78.5 0.1 collective-permute-start.9
  78.6 2.0 %collective-permute-start.8 = (bf16[64,4096]{1,0:T(8,128)(2,1)S(1)}, bf16[64,4096]{1,0:T(8,128)(2,1)S(1)}, u32[]{:S(2)}, u32[]{:S(2)}) collective-permute-start(bf16[64,4096]{1,0:T(8,128)(2,1)S(1)} %slice.30), channel_id=1, source_target_pairs={{0,2},{1,3},{2,4},{3,5},{4,6},{5,7},{6,0},{7,1},{8,10},{9,11},{10,... | collective-permute-start | bytes 1572872 | tf_op jit(solution)/shard_map/ppermute | solution.py:40
  80.6 14.1 %shard_map.78 = (bf16[128,4096]{1,0:T(8,128)(2,1)}, bf16[64,4096]{1,0:T(8,128)(2,1)}, bf16[64,4096]{1,0:T(8,128)(2,1)}, bf16[64,4096]{1,0:T(8,128)(2,1)}, bf16[6...) custom-call(s32[6]{0:T(128)} %stack.23.meta, ...), custom_call_target="tpu_custom_call" | custom-call | flops 1048576 | bytes 65536 | tf_op jit(solution)/shard_map/pallas_call | solution.py:183
  94.7 0.8 copy-done.11
  95.5 0.2 copy-done.12
  95.6 1.3 collective-permute-start.11
  96.9 0.7 collective-permute-start.12
  97.7 11.1 %shard_map.79 = (bf16[64,4096]{1,0:T(8,128)(2,1)}, bf16[64,4096]{1,0:T(8,128)(2,1)}, bf16[128,512]{1,0:T(8,128)(2,1)}, bf16[128,4608]{1,0:T(8,128)(2,1)}) custom-call(s32[6]{0:T(128)} %stack.23.meta, bf16[64,4096]{1,0:T(8,128)(2,1)} %copy-done.12, bf16[64,4096]{1,0:T(8,128)(2,1)} %copy-done.11, bf16[8,128,1024]{2,1,0:T(8,128)(2,1)} %all-to-all-done.refs_4_.refs_3_.refs_2_, ...), custom_call_target="tpu_custom_call" | custom-call | flops 1048576 | bytes 65536 | tf_op jit(solution)/shard_map/pallas_call | solution.py:183
  108.8 1.5 collective-permute-done.11
  110.3 2.1 %collective-permute-done.12 = bf16[64,4096]{1,0:T(8,128)(2,1)S(1)} collective-permute-done((bf16[64,4096]{1,0:T(8,128)(2,1)}, bf16[64,4096]{1,0:T(8,128)(2,1)S(1)}, u32[]{:S(2)}, u32[]{:S(2)}) %collective-permute-start.12) | collective-permute-done | bytes 524320 | tf_op jit(solution)/shard_map/ppermute | solution.py:40
  112.5 0.7 collective-permute-start.15
  113.2 1.6 collective-permute-start.16
  114.8 0.6 collective-permute-start.17
  115.4 0.2 collective-permute-done.14.refs_8_
  115.7 10.8 %shard_map.80 = (bf16[512,512]{1,0:T(8,128)(2,1)}, bf16[512,512]{1,0:T(8,128)(2,1)}, bf16[512,512]{1,0:T(8,128)(2,1)}, bf16[512,512]{1,0:T(8,128)(2,1)}, bf16[4096,512]{1,0:T(8,128)(2,1)}) custom-call(s32[6]{0:T(128)} %stack.23.meta, f32[1]{0:T(128)S(6)} %rsqrt.4.scale.refs_11_, bf16[512,4608]{1,0:T(8,128)(2,1)} %get-tuple-element.74.refs_0_, ...), custom_call_target="tpu_custom_call" | custom-call | flops 1048576 | bytes 65536 | tf_op jit(solution)/shard_map/pallas_call | solution.py:264
  126.5 0.6 collective-permute-done.15
  127.2 1.3 collective-permute-done.16
  128.5 1.6 collective-permute-start.18
  130.1 1.7 collective-permute-start.19
  131.7 1.3 add_convert_fusion.8
  133.0 0.4 collective-permute-start.20
  133.4 1.2 add_convert_fusion.7
  134.6 1.8 collective-permute-start.21
  136.4 10.7 %shard_map.81 = (bf16[512,512]{1,0:T(8,128)(2,1)}, bf16[512,512]{1,0:T(8,128)(2,1)}, bf16[512,512]{1,0:T(8,128)(2,1)}, bf16[512,512]{1,0:T(8,128)(2,1)}, bf16[4096,512]{1,0:T(8,128)(2,1)}) custom-call(s32[6]{0:T(128)} %stack.23.meta, f32[1]{0:T(128)S(6)} %rsqrt.4.scale.refs_11_, ...), custom_call_target="tpu_custom_call", output_to_operand_aliasing={{4}: (13, {})} | custom-call | flops 1048576 | bytes 65536 | tf_op jit(solution)/shard_map/pallas_call | solution.py:264
  147.2 1.2 collective-permute-done.21
  148.3 1.3 fusion.2
  149.6 0.1 add_convert_fusion.6
  149.8 0.4 collective-permute-start.25
  150.1 2.9 %collective-permute-start.26 = (bf16[512,512]{1,0:T(8,128)(2,1)S(1)}, bf16[512,512]{1,0:T(8,128)(2,1)S(1)}, u32[]{:S(2)}, u32[]{:S(2)}) collective-permute-start(bf16[512,512]{1,0:T(8,128)(2,1)S(1)} %copy-done.18), channel_id=1, source_target_pairs={{0,48},{16,0},{32,16},{48,32},{64,112},{80,64},{96,80},{112,96},{1... | collective-permute-start | bytes 1572872 | tf_op jit(solution)/shard_map/ppermute | solution.py:44
  153.1 1.3 add_convert_fusion.3
  154.4 0.8 collective-permute-start.22
  155.1 0.2 add_convert_fusion.2
  155.4 1.6 collective-permute-start.23
  157.0 0.2 add_convert_fusion.1
  157.3 0.9 collective-permute-start.24
  158.2 4.4 %collective-permute-done.25 = bf16[512,512]{1,0:T(8,128)(2,1)S(1)} collective-permute-done((bf16[512,512]{1,0:T(8,128)(2,1)S(1)}, bf16[512,512]{1,0:T(8,128)(2,1)S(1)}, u32[]{:S(2)}, u32[]{:S(2)}) %collective-permute-start.25) | collective-permute-done | bytes 524320 | tf_op jit(solution)/shard_map/ppermute | solution.py:44
  162.6 0.1 add_convert_fusion.5
  162.8 3.0 %collective-permute-start.27 = (bf16[512,512]{1,0:T(8,128)(2,1)S(1)}, bf16[512,512]{1,0:T(8,128)(2,1)S(1)}, u32[]{:S(2)}, u32[]{:S(2)}) collective-permute-start(bf16[512,512]{1,0:T(8,128)(2,1)S(1)} %add_convert_fusion.5), channel_id=1, source_target_pairs={{0,48},{16,0},{32,16},{48,32},{64,112},{80,64},{96,80},{112,96},{1... | collective-permute-start | bytes 1572872 | tf_op jit(solution)/shard_map/ppermute | solution.py:44
  165.8 0.2 add_convert_fusion.4
  166.0 10.9 %collective-permute-done.22 = bf16[128,4096]{1,0:T(8,128)(2,1)S(1)} collective-permute-done((bf16[128,4096]{1,0:T(8,128)(2,1)S(1)}, bf16[128,4096]{1,0:T(8,128)(2,1)S(1)}, u32[]{:S(2)}, u32[]{:S(2)}) %collective-permute-start.22) | collective-permute-done | bytes 1048608 | tf_op jit(solution)/shard_map/ppermute | solution.py:40
  176.9 2.7 %collective-permute-start.29 = (bf16[512,512]{1,0:T(8,128)(2,1)S(1)}, bf16[512,512]{1,0:T(8,128)(2,1)S(1)}, u32[]{:S(2)}, u32[]{:S(2)}) collective-permute-start(bf16[512,512]{1,0:T(8,128)(2,1)S(1)} %add_convert_fusion.4), channel_id=1, source_target_pairs={{0,64},{16,80},{32,96},{48,112},{64,0},{80,16},{96,32},{112,48},{1... | collective-permute-start | bytes 1572872 | tf_op jit(solution)/shard_map/ppermute | solution.py:44
  179.6 1.7 collective-permute-done.24
  181.4 1.6 add_convert_fusion
  183.0 8.8 %collective-permute-done.29 = bf16[512,512]{1,0:T(8,128)(2,1)S(1)} collective-permute-done((bf16[512,512]{1,0:T(8,128)(2,1)S(1)}, bf16[512,512]{1,0:T(8,128)(2,1)S(1)}, u32[]{:S(2)}, u32[]{:S(2)}) %collective-permute-start.29) | collective-permute-done | bytes 524320 | tf_op jit(solution)/shard_map/ppermute | solution.py:44
  191.8 1.2 convert_add_fusion
  (57 shorter events, 0.2 us)
Async XLA Ops:
  0.6 26.5 %collective-permute-start.2 = (bf16[128,4096]{1,0:T(8,128)(2,1)}, bf16[128,4096]{1,0:T(8,128)(2,1)}, u32[]{:S(2)}, u32[]{:S(2)}) collective-permute-start(bf16[128,4096]{1,0:T(8,128)(2,1)} %bitcast.20), channel_id=1, source_target_pairs={{0,8},{1,9},{2,10},{3,11},{4,12},{5,13},{6,14},{7,15},{8,0},{9,1},... | collective-permute-start | bytes 3145736 | tf_op jit(solution)/shard_map/ppermute | solution.py:40
  2.3 39.2 %collective-permute-start.1 = (bf16[128,4096]{1,0:T(8,128)(2,1)}, bf16[128,4096]{1,0:T(8,128)(2,1)S(1)}, u32[]{:S(2)}, u32[]{:S(2)}) collective-permute-start(bf16[128,4096]{1,0:T(8,128)(2,1)} %bitcast.21), channel_id=1, source_target_pairs={{0,6},{1,7},{2,0},{3,1},{4,2},{5,3},{6,4},{7,5},{8,14},{9,15},{10,... | collective-permute-start | bytes 3145736 | tf_op jit(solution)/shard_map/ppermute | solution.py:40
  6.3 44.5 %collective-permute-start = (bf16[128,4096]{1,0:T(8,128)(2,1)}, bf16[128,4096]{1,0:T(8,128)(2,1)}, u32[]{:S(2)}, u32[]{:S(2)}) collective-permute-start(bf16[128,4096]{1,0:T(8,128)(2,1)} %bitcast.22), channel_id=1, source_target_pairs={{0,2},{1,3},{2,4},{3,5},{4,6},{5,7},{6,0},{7,1},{8,10},{9,11},{10,... | collective-permute-start | bytes 3145736 | tf_op jit(solution)/shard_map/ppermute | solution.py:40
  13.7 1.3 copy-start
  13.7 42.7 %collective-permute-start.7 = (bf16[2048,512]{1,0:T(8,128)(2,1)S(1)}, bf16[2048,512]{1,0:T(8,128)(2,1)}, u32[]{:S(2)}, u32[]{:S(2)}) collective-permute-start(bf16[2048,512]{1,0:T(8,128)(2,1)S(1)} %get-tuple-element.135.refs_6_.refs_5_.refs_4_), channel_id=1, source_target_pairs={{0,1},{1,0},{2,3},{3,2},{4,5},{5,4},{6,7},{7,6},{8,9},{9,8},{10,11... | collective-permute-start | bytes 6291464 | tf_op jit(solution)/shard_map/ppermute | solution.py:40
  13.7 42.7 %collective-permute-start.6 = (bf16[2048,512]{1,0:T(8,128)(2,1)}, bf16[2048,512]{1,0:T(8,128)(2,1)}, u32[]{:S(2)}, u32[]{:S(2)}) collective-permute-start(bf16[2048,512]{1,0:T(8,128)(2,1)} %get-tuple-element.136.refs_5_.refs_4_.refs_3_), channel_id=1, source_target_pairs={{0,1},{1,0},{2,3},{3,2},{4,5},{5,4},{6,7},{7,6},{8,9},{9,8},{10,11... | collective-permute-start | bytes 6291464 | tf_op jit(solution)/shard_map/ppermute | solution.py:40
  15.0 41.4 %all-to-all-start = ((bf16[8,128,1024]{2,1,0:T(8,128)(2,1)}), bf16[8,128,1024]{2,1,0:T(8,128)(2,1)}, u32[]{:S(2)}, u32[]{:S(2)}) async-start(bf16[8,128,1024]{2,1,0:T(8,128)(2,1)} %shard_map.76), calls=%async_computation | async-start | bytes 4194304 | tf_op jit(solution)/shard_map/all_to_all | solution.py:315
  41.5 1.0 copy-start.5
  50.8 26.2 %collective-permute-start.3 = (bf16[128,4096]{1,0:T(8,128)(2,1)}, bf16[128,4096]{1,0:T(8,128)(2,1)S(1)}, u32[]{:S(2)}, u32[]{:S(2)}) collective-permute-start(bf16[128,4096]{1,0:T(8,128)(2,1)} %collective-permute-done.2.refs_3_), channel_id=1, source_target_pairs={{0,2},{1,3},{2,4},{3,5},{4,6},{5,7},{6,0},{7,1},{8,10},{9,11},{10,... | collective-permute-start | bytes 3145736 | tf_op jit(solution)/shard_map/ppermute | solution.py:40
  50.8 26.2 %collective-permute-start.5 = (bf16[128,4096]{1,0:T(8,128)(2,1)}, bf16[128,4096]{1,0:T(8,128)(2,1)}, u32[]{:S(2)}, u32[]{:S(2)}) collective-permute-start(bf16[128,4096]{1,0:T(8,128)(2,1)} %copy-done.5), channel_id=1, source_target_pairs={{0,8},{1,9},{2,10},{3,11},{4,12},{5,13},{6,14},{7,15},{8,0},{9,1},... | collective-permute-start | bytes 3145736 | tf_op jit(solution)/shard_map/ppermute | solution.py:40
  51.3 25.7 %collective-permute-start.4 = (bf16[128,4096]{1,0:T(8,128)(2,1)}, bf16[128,4096]{1,0:T(8,128)(2,1)}, u32[]{:S(2)}, u32[]{:S(2)}) collective-permute-start(bf16[128,4096]{1,0:T(8,128)(2,1)} %copy-done.5), channel_id=1, source_target_pairs={{0,6},{1,7},{2,0},{3,1},{4,2},{5,3},{6,4},{7,5},{8,14},{9,15},{10,... | collective-permute-start | bytes 3145736 | tf_op jit(solution)/shard_map/ppermute | solution.py:40
  77.0 3.6 %copy-start.2 = (bf16[128,4096]{1,0:T(8,128)(2,1)}, bf16[128,4096]{1,0:T(8,128)(2,1)S(1)}, u32[]{:S(2)}) copy-start(bf16[128,4096]{1,0:T(8,128)(2,1)S(1)} %collective-permute-done.3.refs_2_) | copy-start | bytes 3145732
  77.0 17.7 %collective-permute-start.10 = (bf16[512,4608]{1,0:T(8,128)(2,1)}, bf16[512,4608]{1,0:T(8,128)(2,1)}, u32[]{:S(2)}, u32[]{:S(2)}) collective-permute-start(bf16[512,4608]{1,0:T(8,128)(2,1)} %get-tuple-element.74.refs_0_), channel_id=1, source_target_pairs={{0,1},{1,0},{2,3},{3,2},{4,5},{5,4},{6,7},{7,6},{8,9},{9,8},{10,11... | collective-permute-start | bytes 14155784 | tf_op jit(solution)/shard_map/ppermute | solution.py:40
  78.5 16.2 %collective-permute-start.9 = (bf16[64,4096]{1,0:T(8,128)(2,1)S(1)}, bf16[64,4096]{1,0:T(8,128)(2,1)S(1)}, u32[]{:S(2)}, u32[]{:S(2)}) collective-permute-start(bf16[64,4096]{1,0:T(8,128)(2,1)S(1)} %slice.31), channel_id=1, source_target_pairs={{0,6},{1,7},{2,0},{3,1},{4,2},{5,3},{6,4},{7,5},{8,14},{9,15},{10,... | collective-permute-start | bytes 1572872 | tf_op jit(solution)/shard_map/ppermute | solution.py:40
  78.6 16.1 %collective-permute-start.8 = (bf16[64,4096]{1,0:T(8,128)(2,1)S(1)}, bf16[64,4096]{1,0:T(8,128)(2,1)S(1)}, u32[]{:S(2)}, u32[]{:S(2)}) collective-permute-start(bf16[64,4096]{1,0:T(8,128)(2,1)S(1)} %slice.30), channel_id=1, source_target_pairs={{0,2},{1,3},{2,4},{3,5},{4,6},{5,7},{6,0},{7,1},{8,10},{9,11},{10,... | collective-permute-start | bytes 1572872 | tf_op jit(solution)/shard_map/ppermute | solution.py:40
  94.7 0.8 copy-start.11
  94.7 0.9 copy-start.12
  95.6 16.8 %collective-permute-start.13 = (bf16[384,4608]{1,0:T(8,128)(2,1)}, bf16[384,4608]{1,0:T(8,128)(2,1)S(1)}, u32[]{:S(2)}, u32[]{:S(2)}) collective-permute-start(bf16[384,4608]{1,0:T(8,128)(2,1)} %get-tuple-element.82.refs_1_), channel_id=1, source_target_pairs={{0,1},{1,0},{2,3},{3,2},{4,5},{5,4},{6,7},{7,6},{8,9},{9,8},{10,11... | collective-permute-start | bytes 10616840 | tf_op jit(solution)/shard_map/ppermute | solution.py:40
  95.6 14.7 %collective-permute-start.11 = (bf16[64,4096]{1,0:T(8,128)(2,1)}, bf16[64,4096]{1,0:T(8,128)(2,1)}, u32[]{:S(2)}, u32[]{:S(2)}) collective-permute-start(bf16[64,4096]{1,0:T(8,128)(2,1)} %get-tuple-element.83), channel_id=1, source_target_pairs={{0,6},{1,7},{2,0},{3,1},{4,2},{5,3},{6,4},{7,5},{8,14},{9,15},{10,... | collective-permute-start | bytes 1572872 | tf_op jit(solution)/shard_map/ppermute | solution.py:40
  96.9 15.5 %collective-permute-start.12 = (bf16[64,4096]{1,0:T(8,128)(2,1)}, bf16[64,4096]{1,0:T(8,128)(2,1)S(1)}, u32[]{:S(2)}, u32[]{:S(2)}) collective-permute-start(bf16[64,4096]{1,0:T(8,128)(2,1)} %get-tuple-element.84), channel_id=1, source_target_pairs={{0,2},{1,3},{2,4},{3,5},{4,6},{5,7},{6,0},{7,1},{8,10},{9,11},{10,... | collective-permute-start | bytes 1572872 | tf_op jit(solution)/shard_map/ppermute | solution.py:40
  112.4 3.3 %copy-start.13 = (bf16[64,4096]{1,0:T(8,128)(2,1)}, bf16[64,4096]{1,0:T(8,128)(2,1)S(1)}, u32[]{:S(2)}) copy-start(bf16[64,4096]{1,0:T(8,128)(2,1)S(1)} %collective-permute-done.12) | copy-start | bytes 1572868
  112.4 3.3 %copy-start.1 = (bf16[384,4608]{1,0:T(8,128)(2,1)}, bf16[384,4608]{1,0:T(8,128)(2,1)S(1)}, u32[]{:S(2)}) copy-start(bf16[384,4608]{1,0:T(8,128)(2,1)S(1)} %collective-permute-done.13.refs_7_) | copy-start | bytes 10616836
  112.4 3.3 %collective-permute-start.14 = (bf16[128,4608]{1,0:T(8,128)(2,1)}, bf16[128,4608]{1,0:T(8,128)(2,1)}, u32[]{:S(2)}, u32[]{:S(2)}) collective-permute-start(bf16[128,4608]{1,0:T(8,128)(2,1)} %get-tuple-element.90.refs_2_), channel_id=1, source_target_pairs={{0,1},{1,0},{2,3},{3,2},{4,5},{5,4},{6,7},{7,6},{8,9},{9,8},{10,11... | collective-permute-start | bytes 3538952 | tf_op jit(solution)/shard_map/ppermute | solution.py:40
  112.5 14.6 %collective-permute-start.15 = (bf16[64,4096]{1,0:T(8,128)(2,1)}, bf16[64,4096]{1,0:T(8,128)(2,1)}, u32[]{:S(2)}, u32[]{:S(2)}) collective-permute-start(bf16[64,4096]{1,0:T(8,128)(2,1)} %get-tuple-element.96), channel_id=1, source_target_pairs={{0,6},{1,7},{2,0},{3,1},{4,2},{5,3},{6,4},{7,5},{8,14},{9,15},{10,... | collective-permute-start | bytes 1572872 | tf_op jit(solution)/shard_map/ppermute | solution.py:40
  113.2 15.3 %collective-permute-start.16 = (bf16[64,4096]{1,0:T(8,128)(2,1)}, bf16[64,4096]{1,0:T(8,128)(2,1)}, u32[]{:S(2)}, u32[]{:S(2)}) collective-permute-start(bf16[64,4096]{1,0:T(8,128)(2,1)} %get-tuple-element.97), channel_id=1, source_target_pairs={{0,2},{1,3},{2,4},{3,5},{4,6},{5,7},{6,0},{7,1},{8,10},{9,11},{10,... | collective-permute-start | bytes 1572872 | tf_op jit(solution)/shard_map/ppermute | solution.py:40
  114.8 32.3 %collective-permute-start.17 = (bf16[128,4096]{1,0:T(8,128)(2,1)}, bf16[128,4096]{1,0:T(8,128)(2,1)}, u32[]{:S(2)}, u32[]{:S(2)}) collective-permute-start(bf16[128,4096]{1,0:T(8,128)(2,1)} %get-tuple-element.107), channel_id=1, source_target_pairs={{0,8},{1,9},{2,10},{3,11},{4,12},{5,13},{6,14},{7,15},{8,0},{9,1},... | collective-permute-start | bytes 3145736 | tf_op jit(solution)/shard_map/ppermute | solution.py:40
  115.7 17.7 %copy-start.8 = (bf16[64,4096]{1,0:T(8,128)(2,1)S(1)}, bf16[64,4096]{1,0:T(8,128)(2,1)}, u32[]{:S(2)}) copy-start(bf16[64,4096]{1,0:T(8,128)(2,1)} %get-tuple-element.112) | copy-start | bytes 1572868
  128.5 18.6 %collective-permute-start.18 = (bf16[512,512]{1,0:T(8,128)(2,1)}, bf16[512,512]{1,0:T(8,128)(2,1)S(1)}, u32[]{:S(2)}, u32[]{:S(2)}) collective-permute-start(bf16[512,512]{1,0:T(8,128)(2,1)} %get-tuple-element.108), channel_id=1, source_target_pairs={{0,16},{16,32},{32,48},{48,0},{64,80},{80,96},{96,112},{112,64},{1... | collective-permute-start | bytes 1572872 | tf_op jit(solution)/shard_map/ppermute | solution.py:44
  130.1 17.1 %collective-permute-start.19 = (bf16[512,512]{1,0:T(8,128)(2,1)}, bf16[512,512]{1,0:T(8,128)(2,1)S(1)}, u32[]{:S(2)}, u32[]{:S(2)}) collective-permute-start(bf16[512,512]{1,0:T(8,128)(2,1)} %get-tuple-element.109), channel_id=1, source_target_pairs={{0,48},{16,0},{32,16},{48,32},{64,112},{80,64},{96,80},{112,96},{1... | collective-permute-start | bytes 1572872 | tf_op jit(solution)/shard_map/ppermute | solution.py:44
  133.0 14.1 %collective-permute-start.20 = (bf16[64,4096]{1,0:T(8,128)(2,1)S(1)}, bf16[64,4096]{1,0:T(8,128)(2,1)S(1)}, u32[]{:S(2)}, u32[]{:S(2)}) collective-permute-start(bf16[64,4096]{1,0:T(8,128)(2,1)S(1)} %add_convert_fusion.8), channel_id=1, source_target_pairs={{0,6},{1,7},{2,0},{3,1},{4,2},{5,3},{6,4},{7,5},{8,14},{9,15},{10,... | collective-permute-start | bytes 1572872 | tf_op jit(solution)/shard_map/ppermute | solution.py:40
  134.6 13.8 %collective-permute-start.21 = (bf16[64,4096]{1,0:T(8,128)(2,1)S(1)}, bf16[64,4096]{1,0:T(8,128)(2,1)S(1)}, u32[]{:S(2)}, u32[]{:S(2)}) collective-permute-start(bf16[64,4096]{1,0:T(8,128)(2,1)S(1)} %add_convert_fusion.7), channel_id=1, source_target_pairs={{0,2},{1,3},{2,4},{3,5},{4,6},{5,7},{6,0},{7,1},{8,10},{9,11},{10,... | collective-permute-start | bytes 1572872 | tf_op jit(solution)/shard_map/ppermute | solution.py:40
  147.1 2.5 %copy-start.10 = (bf16[512,512]{1,0:T(8,128)(2,1)S(1)}, bf16[512,512]{1,0:T(8,128)(2,1)}, u32[]{:S(2)}) copy-start(bf16[512,512]{1,0:T(8,128)(2,1)} %get-tuple-element.125) | copy-start | bytes 1572868
  147.1 3.1 %copy-start.18 = (bf16[512,512]{1,0:T(8,128)(2,1)S(1)}, bf16[512,512]{1,0:T(8,128)(2,1)}, u32[]{:S(2)}) copy-start(bf16[512,512]{1,0:T(8,128)(2,1)} %get-tuple-element.127) | copy-start | bytes 1572868
  147.1 6.0 %copy-start.7 = (bf16[128,4096]{1,0:T(8,128)(2,1)S(1)}, bf16[128,4096]{1,0:T(8,128)(2,1)}, u32[]{:S(2)}) copy-start(bf16[128,4096]{1,0:T(8,128)(2,1)} %get-tuple-element.105) | copy-start | bytes 3145732
  149.6 5.5 %copy-start.6 = (bf16[128,4096]{1,0:T(8,128)(2,1)S(1)}, bf16[128,4096]{1,0:T(8,128)(2,1)}, u32[]{:S(2)}) copy-start(bf16[128,4096]{1,0:T(8,128)(2,1)} %get-tuple-element.118) | copy-start | bytes 3145732
  149.6 5.5 %copy-start.14 = (bf16[64,4096]{1,0:T(8,128)(2,1)S(1)}, bf16[64,4096]{1,0:T(8,128)(2,1)}, u32[]{:S(2)}) copy-start(bf16[64,4096]{1,0:T(8,128)(2,1)} %copy-done.13) | copy-start | bytes 1572868
  149.8 12.8 %collective-permute-start.25 = (bf16[512,512]{1,0:T(8,128)(2,1)S(1)}, bf16[512,512]{1,0:T(8,128)(2,1)S(1)}, u32[]{:S(2)}, u32[]{:S(2)}) collective-permute-start(bf16[512,512]{1,0:T(8,128)(2,1)S(1)} %add_convert_fusion.6), channel_id=1, source_target_pairs={{0,16},{16,32},{32,48},{48,0},{64,80},{80,96},{96,112},{112,64},{1... | collective-permute-start | bytes 1572872 | tf_op jit(solution)/shard_map/ppermute | solution.py:44
  150.1 12.5 %collective-permute-start.26 = (bf16[512,512]{1,0:T(8,128)(2,1)S(1)}, bf16[512,512]{1,0:T(8,128)(2,1)S(1)}, u32[]{:S(2)}, u32[]{:S(2)}) collective-permute-start(bf16[512,512]{1,0:T(8,128)(2,1)S(1)} %copy-done.18), channel_id=1, source_target_pairs={{0,48},{16,0},{32,16},{48,32},{64,112},{80,64},{96,80},{112,96},{1... | collective-permute-start | bytes 1572872 | tf_op jit(solution)/shard_map/ppermute | solution.py:44
  154.4 2.7 %copy-start.4 = (bf16[128,4096]{1,0:T(8,128)(2,1)S(1)}, bf16[128,4096]{1,0:T(8,128)(2,1)}, u32[]{:S(2)}) copy-start(bf16[128,4096]{1,0:T(8,128)(2,1)} %get-tuple-element.120) | copy-start | bytes 3145732
  154.4 22.5 %collective-permute-start.22 = (bf16[128,4096]{1,0:T(8,128)(2,1)S(1)}, bf16[128,4096]{1,0:T(8,128)(2,1)S(1)}, u32[]{:S(2)}, u32[]{:S(2)}) collective-permute-start(bf16[128,4096]{1,0:T(8,128)(2,1)S(1)} %add_convert_fusion.3), channel_id=1, source_target_pairs={{0,6},{1,7},{2,0},{3,1},{4,2},{5,3},{6,4},{7,5},{8,14},{9,15},{10,... | collective-permute-start | bytes 3145736 | tf_op jit(solution)/shard_map/ppermute | solution.py:40
  155.4 7.2 %copy-start.9 = (bf16[512,512]{1,0:T(8,128)(2,1)S(1)}, bf16[512,512]{1,0:T(8,128)(2,1)}, u32[]{:S(2)}) copy-start(bf16[512,512]{1,0:T(8,128)(2,1)} %get-tuple-element.124) | copy-start | bytes 1572868
  155.4 24.2 %collective-permute-start.23 = (bf16[128,4096]{1,0:T(8,128)(2,1)S(1)}, bf16[128,4096]{1,0:T(8,128)(2,1)S(1)}, u32[]{:S(2)}, u32[]{:S(2)}) collective-permute-start(bf16[128,4096]{1,0:T(8,128)(2,1)S(1)} %add_convert_fusion.2), channel_id=1, source_target_pairs={{0,2},{1,3},{2,4},{3,5},{4,6},{5,7},{6,0},{7,1},{8,10},{9,11},{10,... | collective-permute-start | bytes 3145736 | tf_op jit(solution)/shard_map/ppermute | solution.py:40
  157.0 8.7 %copy-start.17 = (bf16[512,512]{1,0:T(8,128)(2,1)S(1)}, bf16[512,512]{1,0:T(8,128)(2,1)}, u32[]{:S(2)}) copy-start(bf16[512,512]{1,0:T(8,128)(2,1)} %get-tuple-element.130) | copy-start | bytes 1572868
  157.0 8.7 %copy-start.16 = (bf16[512,512]{1,0:T(8,128)(2,1)S(1)}, bf16[512,512]{1,0:T(8,128)(2,1)}, u32[]{:S(2)}) copy-start(bf16[512,512]{1,0:T(8,128)(2,1)} %get-tuple-element.131) | copy-start | bytes 1572868
  157.3 24.1 %copy-start.3 = (bf16[128,4096]{1,0:T(8,128)(2,1)S(1)}, bf16[128,4096]{1,0:T(8,128)(2,1)}, u32[]{:S(2)}) copy-start(bf16[128,4096]{1,0:T(8,128)(2,1)} %get-tuple-element.104) | copy-start | bytes 3145732
  157.3 24.1 %collective-permute-start.24 = (bf16[128,4096]{1,0:T(8,128)(2,1)S(1)}, bf16[128,4096]{1,0:T(8,128)(2,1)S(1)}, u32[]{:S(2)}, u32[]{:S(2)}) collective-permute-start(bf16[128,4096]{1,0:T(8,128)(2,1)S(1)} %add_convert_fusion.1), channel_id=1, source_target_pairs={{0,8},{1,9},{2,10},{3,11},{4,12},{5,13},{6,14},{7,15},{8,0},{9,1},... | collective-permute-start | bytes 3145736 | tf_op jit(solution)/shard_map/ppermute | solution.py:40
  162.8 20.3 %collective-permute-start.27 = (bf16[512,512]{1,0:T(8,128)(2,1)S(1)}, bf16[512,512]{1,0:T(8,128)(2,1)S(1)}, u32[]{:S(2)}, u32[]{:S(2)}) collective-permute-start(bf16[512,512]{1,0:T(8,128)(2,1)S(1)} %add_convert_fusion.5), channel_id=1, source_target_pairs={{0,48},{16,0},{32,16},{48,32},{64,112},{80,64},{96,80},{112,96},{1... | collective-permute-start | bytes 1572872 | tf_op jit(solution)/shard_map/ppermute | solution.py:44
  165.8 17.3 %collective-permute-start.28 = (bf16[512,512]{1,0:T(8,128)(2,1)S(1)}, bf16[512,512]{1,0:T(8,128)(2,1)S(1)}, u32[]{:S(2)}, u32[]{:S(2)}) collective-permute-start(bf16[512,512]{1,0:T(8,128)(2,1)S(1)} %copy-done.17), channel_id=1, source_target_pairs={{0,16},{16,32},{32,48},{48,0},{64,80},{80,96},{96,112},{112,64},{1... | collective-permute-start | bytes 1572872 | tf_op jit(solution)/shard_map/ppermute | solution.py:44
  176.9 14.9 %collective-permute-start.29 = (bf16[512,512]{1,0:T(8,128)(2,1)S(1)}, bf16[512,512]{1,0:T(8,128)(2,1)S(1)}, u32[]{:S(2)}, u32[]{:S(2)}) collective-permute-start(bf16[512,512]{1,0:T(8,128)(2,1)S(1)} %add_convert_fusion.4), channel_id=1, source_target_pairs={{0,64},{16,80},{32,96},{48,112},{64,0},{80,16},{96,32},{112,48},{1... | collective-permute-start | bytes 1572872 | tf_op jit(solution)/shard_map/ppermute | solution.py:44
  181.4 10.5 %copy-start.15 = (bf16[512,512]{1,0:T(8,128)(2,1)S(1)}, bf16[512,512]{1,0:T(8,128)(2,1)}, u32[]{:S(2)}) copy-start(bf16[512,512]{1,0:T(8,128)(2,1)} %get-tuple-element.123) | copy-start | bytes 1572868

commit v2 on v1

--- a/solution.py
+++ b/solution.py
@@ -310,7 +310,7 @@
     h_at, y_at = dom // NY, dom % NY
 
     meta = jnp.stack([live, core, x_at, z_at, h_at, y_at]).astype(jnp.int32)
-    m1, p1, q0 = send(rows_in, dz=1), send(rows_in, dz=-1), send(rows_in, dx=1)
+    q0, p1, m1 = send(rows_in, dx=1), send(rows_in, dz=-1), send(rows_in, dz=1)
     chunks = split_cotangent(cotangent[0])
     cot = lax.all_to_all(
         chunks,
@@ -326,8 +326,8 @@
         for h in (0, D // 2)
     ]
     eff += [send(part, dc=1) for part in eff]
-    m1, p1, q0 = together(m1, p1, q0)
-    qm, o2, qp = send(q0, dz=1), send(p1, dz=-1), send(p1, dx=1)
+    q0, p1, m1 = together(q0, p1, m1)
+    qp, o2, qm = send(p1, dx=1), send(p1, dz=-1), send(q0, dz=1)
 
     common = (eff, cot, meta)
     (d_own, d_m1, d_p1, d_q0), g_near, x_near = block_pass(
@@ -391,6 +391,7 @@
     end_a = send(add(d_m1, jnp.concatenate([o2_right, from_across[HALF:]])), dz=-1)
     end_b = send(add(d_p1, jnp.concatenate([from_across[:HALF], o2_left])), dz=1)
     right0, far1, right1 = together(right0, far1, right1)
+    right1, end_a = together(right1, end_a)
     right1 = send_dom(right1, dy=1)
     left1 = send_dom(add(left1, far1), dy=-1)
     given = send_dom(add(mine0, left0, right0), dh=1)

time: 194 us -> 195 us (level)
  starting transfers between devices: 39.4 us -> 44.4 us
  waiting for transfers between devices: 67.7 us -> 63.9 us
    all_to_all x1, waiting for transfers between devices: 0.56 us -> 15.2 us  [body(): lax.all_to_all(chunks, 'fsdp', split_axis=0, concat_axis=0, tiled=True, a...]
    ppermute x23, waiting for transfers between devices: 53.9 us -> 40.2 us  [send(): return lax.ppermute(value, 'fsdp', fsdp_pairs(dx, dz, dc))]
    ppermute x23, starting transfers between devices: 22.6 us -> 27.4 us  [send(): return lax.ppermute(value, 'fsdp', fsdp_pairs(dx, dz, dc))]
    ppermute x7, waiting for transfers between devices: 13.2 us -> 8.52 us  [send_dom(): return lax.ppermute(value, 'dom', dom_pairs(dh, dy))]
where the time goes in v2:
time: 195 us; the launch traced here: 194 us
  Pallas kernels  65.8 us (34%)
  waiting for transfers between devices  63.9 us (33%)
  starting transfers between devices  44.4 us (23%)
  other arithmetic  12.7 us (7%)
  local copies, waits for them, and re-layouts  5.68 us (3%)
    pallas_call x3, Pallas kernels, block_pass(): pl.pallas_call(functools.partial(block_kernel, pieces, tuple(out_map)), o...  41.8 us
    ppermute x23, waiting for transfers between devices, send(): return lax.ppermute(value, 'fsdp', fsdp_pairs(dx, dz, dc))  40.2 us
    ppermute x23, starting transfers between devices, send(): return lax.ppermute(value, 'fsdp', fsdp_pairs(dx, dz, dc))  27.4 us
    pallas_call x2, Pallas kernels, weight_pass(): pl.pallas_call(functools.partial(weight_kernel, n, dh), in_specs=[pl.Bloc...  21.5 us
    all_to_all x1, waiting for transfers between devices, body(): lax.all_to_all(chunks, 'fsdp', split_axis=0, concat_axis=0, tiled=True, a...  15.2 us
    ppermute x7, starting transfers between devices, send_dom(): return lax.ppermute(value, 'dom', dom_pairs(dh, dy))  12.6 us
    ppermute x7, waiting for transfers between devices, send_dom(): return lax.ppermute(value, 'dom', dom_pairs(dh, dy))  8.52 us
    convert_element_type x9, other arithmetic, add(): return sum((t.astype(F32) for t in terms)).astype(BF)  6.51 us
  transfers between devices with their start and end apart: 31, of which 15 were waited for; matrix products, arithmetic and copies ran while one was open for 7% of the time, Pallas kernels for 34%

profile of v2, /device:TPU:0, one launch (start us, length us, event | category | flops | bytes accessed | tf_op | source)
XLA Modules:
  0.0 194.1 jit_solution(938405581104479492)
XLA Ops:
  0.6 2.1 %collective-permute-start.2 = (bf16[128,4096]{1,0:T(8,128)(2,1)}, bf16[128,4096]{1,0:T(8,128)(2,1)}, u32[]{:S(2)}, u32[]{:S(2)}) collective-permute-start(bf16[128,4096]{1,0:T(8,128)(2,1)} %bitcast.20), channel_id=1, source_target_pairs={{0,2},{1,3},{2,4},{3,5},{4,6},{5,7},{6,0},{7,1},{8,10},{9,11},{10,... | collective-permute-start | bytes 3145736 | tf_op jit(solution)/shard_map/ppermute | solution.py:40
  2.7 2.2 %collective-permute-start.1 = (bf16[128,4096]{1,0:T(8,128)(2,1)}, bf16[128,4096]{1,0:T(8,128)(2,1)S(1)}, u32[]{:S(2)}, u32[]{:S(2)}) collective-permute-start(bf16[128,4096]{1,0:T(8,128)(2,1)} %bitcast.21), channel_id=1, source_target_pairs={{0,6},{1,7},{2,0},{3,1},{4,2},{5,3},{6,4},{7,5},{8,14},{9,15},{10,... | collective-permute-start | bytes 3145736 | tf_op jit(solution)/shard_map/ppermute | solution.py:40
  4.9 1.5 collective-permute-start
  6.4 2.4 %shard_map.76 = bf16[8,128,1024]{2,1,0:T(8,128)(2,1)} custom-call(bf16[128,8192]{1,0:T(8,128)(2,1)} %bitcast.19), custom_call_target="tpu_custom_call" | custom-call | flops 1048576 | bytes 65536 | tf_op jit(solution)/shard_map/pallas_call | solution.py:73
  8.8 5.0 %fusion = (bf16[2048,512]{1,0:T(8,128)(2,1)S(1)}, bf16[2048,512]{1,0:T(8,128)(2,1)}) fusion(bf16[1,4096,512]{2,1,0:T(8,128)(2,1)} %param.8, bf16[4096,512]{1,0:T(8,128)(2,1)} %refs_9_.3), kind=kLoop, calls=%fused_computation.1 | loop fusion | flops 8388608 | bytes 12582912 | tf_op jit(solution)/shard_map/convert_element_type | solution.py:325
  13.8 0.5 collective-permute-start.6
  14.3 0.8 copy-done
  15.1 4.3 %all-to-all-start = ((bf16[8,128,1024]{2,1,0:T(8,128)(2,1)}), bf16[8,128,1024]{2,1,0:T(8,128)(2,1)}, u32[]{:S(2)}, u32[]{:S(2)}) async-start(bf16[8,128,1024]{2,1,0:T(8,128)(2,1)} %shard_map.76), calls=%async_computation | async-start | bytes 4194304 | tf_op jit(solution)/shard_map/all_to_all | solution.py:315
  19.4 10.5 %collective-permute-done.2.refs_1_ = bf16[128,4096]{1,0:T(8,128)(2,1)} collective-permute-done((bf16[128,4096]{1,0:T(8,128)(2,1)}, bf16[128,4096]{1,0:T(8,128)(2,1)}, u32[]{:S(2)}, u32[]{:S(2)}) %collective-permute-start.2) | collective-permute-done | bytes 1048608 | tf_op jit(solution)/shard_map/ppermute | solution.py:40
  29.9 0.6 collective-permute-done.1.refs_2_
  30.6 1.0 copy-done.5
  31.5 4.4 %collective-permute-start.3 = (bf16[128,4096]{1,0:T(8,128)(2,1)}, bf16[128,4096]{1,0:T(8,128)(2,1)S(1)}, u32[]{:S(2)}, u32[]{:S(2)}) collective-permute-start(bf16[128,4096]{1,0:T(8,128)(2,1)} %collective-permute-done.refs_3_), channel_id=1, source_target_pairs={{0,2},{1,3},{2,4},{3,5},{4,6},{5,7},{6,0},{7,1},{8,10},{9,11},{10,... | collective-permute-start | bytes 3145736 | tf_op jit(solution)/shard_map/ppermute | solution.py:40
  36.0 1.5 collective-permute-start.5
  38.1 0.7 stack.23.meta
  38.8 15.2 %all-to-all-done.refs_4_.refs_3_.refs_2_ = bf16[8,128,1024]{2,1,0:T(8,128)(2,1)} async-done(((bf16[8,128,1024]{2,1,0:T(8,128)(2,1)}), bf16[8,128,1024]{2,1,0:T(8,128)(2,1)}, u32[]{:S(2)}, u32[]{:S(2)}) %all-to-all-start) | async-done | bytes 2097184 | tf_op jit(solution)/shard_map/all_to_all | solution.py:315
  54.0 16.7 %shard_map.77 = (bf16[128,4096]{1,0:T(8,128)(2,1)}, bf16[128,4096]{1,0:T(8,128)(2,1)}, bf16[128,4096]{1,0:T(8,128)(2,1)}, bf16[128,4096]{1,0:T(8,128)(2,1)}, bf1...) custom-call(s32[6]{0:T(128)} %stack.23.meta, bf16[128,4096]{1,0:T(8,128)(2,1)} %bitcast.23, ...), custom_call_target="tpu_custom_call" | custom-call | flops 1048576 | bytes 65536 | tf_op jit(solution)/shard_map/pallas_call | solution.py:183
  70.7 2.4 %collective-permute-done.3.refs_2_ = bf16[128,4096]{1,0:T(8,128)(2,1)S(1)} collective-permute-done((bf16[128,4096]{1,0:T(8,128)(2,1)}, bf16[128,4096]{1,0:T(8,128)(2,1)S(1)}, u32[]{:S(2)}, u32[]{:S(2)}) %collective-permute-start.3) | collective-permute-done | bytes 1048608 | tf_op jit(solution)/shard_map/ppermute | solution.py:40
  73.1 1.9 collective-permute-done.5.refs_0_
  75.0 1.1 slice.31
  76.1 1.6 collective-permute-start.9
  77.7 0.5 collective-permute-start.8
  78.2 14.1 %shard_map.78 = (bf16[128,4096]{1,0:T(8,128)(2,1)}, bf16[64,4096]{1,0:T(8,128)(2,1)}, bf16[64,4096]{1,0:T(8,128)(2,1)}, bf16[64,4096]{1,0:T(8,128)(2,1)}, bf16[6...) custom-call(s32[6]{0:T(128)} %stack.23.meta, ...), custom_call_target="tpu_custom_call" | custom-call | flops 1048576 | bytes 65536 | tf_op jit(solution)/shard_map/pallas_call | solution.py:183
  92.3 0.6 collective-permute-done.8.refs_0_
  93.0 0.2 copy-done.11
  93.1 0.6 copy-done.12
  93.7 2.2 %collective-permute-start.11 = (bf16[64,4096]{1,0:T(8,128)(2,1)}, bf16[64,4096]{1,0:T(8,128)(2,1)S(1)}, u32[]{:S(2)}, u32[]{:S(2)}) collective-permute-start(bf16[64,4096]{1,0:T(8,128)(2,1)} %get-tuple-element.85), channel_id=1, source_target_pairs={{0,6},{1,7},{2,0},{3,1},{4,2},{5,3},{6,4},{7,5},{8,14},{9,15},{10,... | collective-permute-start | bytes 1572872 | tf_op jit(solution)/shard_map/ppermute | solution.py:40
  96.0 11.1 %shard_map.79 = (bf16[64,4096]{1,0:T(8,128)(2,1)}, bf16[64,4096]{1,0:T(8,128)(2,1)}, bf16[128,512]{1,0:T(8,128)(2,1)}, bf16[128,4608]{1,0:T(8,128)(2,1)}) custom-call(s32[6]{0:T(128)} %stack.23.meta, bf16[64,4096]{1,0:T(8,128)(2,1)} %copy-done.12, bf16[64,4096]{1,0:T(8,128)(2,1)} %copy-done.11, bf16[8,128,1024]{2,1,0:T(8,128)(2,1)} %all-to-all-done.refs_4_.refs_3_.refs_2_, ...), custom_call_target="tpu_custom_call" | custom-call | flops 1048576 | bytes 65536 | tf_op jit(solution)/shard_map/pallas_call | solution.py:183
  107.1 1.2 collective-permute-done.11
  108.3 3.3 %collective-permute-done.12 = bf16[64,4096]{1,0:T(8,128)(2,1)} collective-permute-done((bf16[64,4096]{1,0:T(8,128)(2,1)}, bf16[64,4096]{1,0:T(8,128)(2,1)}, u32[]{:S(2)}, u32[]{:S(2)}) %collective-permute-start.12) | collective-permute-done | bytes 524320 | tf_op jit(solution)/shard_map/ppermute | solution.py:40
  111.6 0.5 collective-permute-start.15
  112.1 1.7 collective-permute-start.16
  113.9 1.6 collective-permute-start.17
  115.5 10.9 %shard_map.80 = (bf16[512,512]{1,0:T(8,128)(2,1)}, bf16[512,512]{1,0:T(8,128)(2,1)}, bf16[512,512]{1,0:T(8,128)(2,1)}, bf16[512,512]{1,0:T(8,128)(2,1)}, bf16[4096,512]{1,0:T(8,128)(2,1)}) custom-call(s32[6]{0:T(128)} %stack.23.meta, f32[1]{0:T(128)S(6)} %rsqrt.4.scale.refs_11_, bf16[512,4608]{1,0:T(8,128)(2,1)} %get-tuple-element.76.refs_0_, ...), custom_call_target="tpu_custom_call" | custom-call | flops 1048576 | bytes 65536 | tf_op jit(solution)/shard_map/pallas_call | solution.py:264
  126.3 1.1 collective-permute-done.16
  127.4 1.6 collective-permute-start.18
  129.0 1.7 collective-permute-start.19
  130.7 1.3 add_convert_fusion.8
  132.0 0.5 collective-permute-start.20
  132.5 1.2 add_convert_fusion.7
  133.7 1.6 collective-permute-start.21
  135.3 10.7 %shard_map.81 = (bf16[512,512]{1,0:T(8,128)(2,1)}, bf16[512,512]{1,0:T(8,128)(2,1)}, bf16[512,512]{1,0:T(8,128)(2,1)}, bf16[512,512]{1,0:T(8,128)(2,1)}, bf16[4096,512]{1,0:T(8,128)(2,1)}) custom-call(s32[6]{0:T(128)} %stack.23.meta, f32[1]{0:T(128)S(6)} %rsqrt.4.scale.refs_11_, ...), custom_call_target="tpu_custom_call", output_to_operand_aliasing={{4}: (13, {})} | custom-call | flops 1048576 | bytes 65536 | tf_op jit(solution)/shard_map/pallas_call | solution.py:264
  146.1 1.4 collective-permute-done.21
  147.5 0.1 add_convert_fusion.6
  147.7 0.3 collective-permute-start.22
  148.0 3.0 %collective-permute-start.23 = (bf16[512,512]{1,0:T(8,128)(2,1)}, bf16[512,512]{1,0:T(8,128)(2,1)S(1)}, u32[]{:S(2)}, u32[]{:S(2)}) collective-permute-start(bf16[512,512]{1,0:T(8,128)(2,1)} %get-tuple-element.119), channel_id=1, source_target_pairs={{0,48},{16,0},{32,16},{48,32},{64,112},{80,64},{96,80},{112,96},{1... | collective-permute-start | bytes 1572872 | tf_op jit(solution)/shard_map/ppermute | solution.py:44
  151.0 1.3 fusion.2
  152.3 1.4 add_convert_fusion.2
  153.7 0.3 collective-permute-start.25
  154.0 0.2 add_convert_fusion.3
  154.3 3.3 %collective-permute-start.24 = (bf16[128,4096]{1,0:T(8,128)(2,1)S(1)}, bf16[128,4096]{1,0:T(8,128)(2,1)S(1)}, u32[]{:S(2)}, u32[]{:S(2)}) collective-permute-start(bf16[128,4096]{1,0:T(8,128)(2,1)S(1)} %add_convert_fusion.3), channel_id=1, source_target_pairs={{0,6},{1,7},{2,0},{3,1},{4,2},{5,3},{6,4},{7,5},{8,14},{9,15},{10,... | collective-permute-start | bytes 3145736 | tf_op jit(solution)/shard_map/ppermute | solution.py:40
  157.6 0.2 add_convert_fusion.1
  157.8 0.0 copy-start.3
  157.9 1.3 collective-permute-start.26
  159.2 1.3 collective-permute-done.22
  160.5 0.1 add_convert_fusion.5
  160.7 3.2 %collective-permute-start.27 = (bf16[512,512]{1,0:T(8,128)(2,1)S(1)}, bf16[512,512]{1,0:T(8,128)(2,1)S(1)}, u32[]{:S(2)}, u32[]{:S(2)}) collective-permute-start(bf16[512,512]{1,0:T(8,128)(2,1)S(1)} %add_convert_fusion.5), channel_id=1, source_target_pairs={{0,48},{16,0},{32,16},{48,32},{64,112},{80,64},{96,80},{112,96},{1... | collective-permute-start | bytes 1572872 | tf_op jit(solution)/shard_map/ppermute | solution.py:44
  163.9 0.2 add_convert_fusion.4
  164.1 2.8 %collective-permute-start.29 = (bf16[512,512]{1,0:T(8,128)(2,1)S(1)}, bf16[512,512]{1,0:T(8,128)(2,1)S(1)}, u32[]{:S(2)}, u32[]{:S(2)}) collective-permute-start(bf16[512,512]{1,0:T(8,128)(2,1)S(1)} %add_convert_fusion.4), channel_id=1, source_target_pairs={{0,64},{16,80},{32,96},{48,112},{64,0},{80,16},{96,32},{112,48},{1... | collective-permute-start | bytes 1572872 | tf_op jit(solution)/shard_map/ppermute | solution.py:44
  167.0 10.1 %collective-permute-done.24 = bf16[128,4096]{1,0:T(8,128)(2,1)S(1)} collective-permute-done((bf16[128,4096]{1,0:T(8,128)(2,1)S(1)}, bf16[128,4096]{1,0:T(8,128)(2,1)S(1)}, u32[]{:S(2)}, u32[]{:S(2)}) %collective-permute-start.24) | collective-permute-done | bytes 1048608 | tf_op jit(solution)/shard_map/ppermute | solution.py:40
  177.1 0.4 collective-permute-done.25
  177.5 6.6 %collective-permute-done.26 = bf16[128,4096]{1,0:T(8,128)(2,1)S(1)} collective-permute-done((bf16[128,4096]{1,0:T(8,128)(2,1)S(1)}, bf16[128,4096]{1,0:T(8,128)(2,1)S(1)}, u32[]{:S(2)}, u32[]{:S(2)}) %collective-permute-start.26) | collective-permute-done | bytes 1048608 | tf_op jit(solution)/shard_map/ppermute | solution.py:40
  184.0 1.6 add_convert_fusion
  185.7 7.2 %collective-permute-done.29 = bf16[512,512]{1,0:T(8,128)(2,1)S(1)} collective-permute-done((bf16[512,512]{1,0:T(8,128)(2,1)S(1)}, bf16[512,512]{1,0:T(8,128)(2,1)S(1)}, u32[]{:S(2)}, u32[]{:S(2)}) %collective-permute-start.29) | collective-permute-done | bytes 524320 | tf_op jit(solution)/shard_map/ppermute | solution.py:44
  192.9 1.2 convert_add_fusion
  (55 shorter events, 0.2 us)
Async XLA Ops:
  0.6 29.3 %collective-permute-start.2 = (bf16[128,4096]{1,0:T(8,128)(2,1)}, bf16[128,4096]{1,0:T(8,128)(2,1)}, u32[]{:S(2)}, u32[]{:S(2)}) collective-permute-start(bf16[128,4096]{1,0:T(8,128)(2,1)} %bitcast.20), channel_id=1, source_target_pairs={{0,2},{1,3},{2,4},{3,5},{4,6},{5,7},{6,0},{7,1},{8,10},{9,11},{10,... | collective-permute-start | bytes 3145736 | tf_op jit(solution)/shard_map/ppermute | solution.py:40
  2.7 27.9 %collective-permute-start.1 = (bf16[128,4096]{1,0:T(8,128)(2,1)}, bf16[128,4096]{1,0:T(8,128)(2,1)S(1)}, u32[]{:S(2)}, u32[]{:S(2)}) collective-permute-start(bf16[128,4096]{1,0:T(8,128)(2,1)} %bitcast.21), channel_id=1, source_target_pairs={{0,6},{1,7},{2,0},{3,1},{4,2},{5,3},{6,4},{7,5},{8,14},{9,15},{10,... | collective-permute-start | bytes 3145736 | tf_op jit(solution)/shard_map/ppermute | solution.py:40
  4.9 26.6 %collective-permute-start = (bf16[128,4096]{1,0:T(8,128)(2,1)}, bf16[128,4096]{1,0:T(8,128)(2,1)}, u32[]{:S(2)}, u32[]{:S(2)}) collective-permute-start(bf16[128,4096]{1,0:T(8,128)(2,1)} %bitcast.22), channel_id=1, source_target_pairs={{0,8},{1,9},{2,10},{3,11},{4,12},{5,13},{6,14},{7,15},{8,0},{9,1},... | collective-permute-start | bytes 3145736 | tf_op jit(solution)/shard_map/ppermute | solution.py:40
  13.8 1.3 copy-start
  13.8 40.2 %collective-permute-start.7 = (bf16[2048,512]{1,0:T(8,128)(2,1)S(1)}, bf16[2048,512]{1,0:T(8,128)(2,1)}, u32[]{:S(2)}, u32[]{:S(2)}) collective-permute-start(bf16[2048,512]{1,0:T(8,128)(2,1)S(1)} %get-tuple-element.139.refs_6_.refs_5_.refs_4_), channel_id=1, source_target_pairs={{0,1},{1,0},{2,3},{3,2},{4,5},{5,4},{6,7},{7,6},{8,9},{9,8},{10,11... | collective-permute-start | bytes 6291464 | tf_op jit(solution)/shard_map/ppermute | solution.py:40
  13.8 40.2 %collective-permute-start.6 = (bf16[2048,512]{1,0:T(8,128)(2,1)}, bf16[2048,512]{1,0:T(8,128)(2,1)}, u32[]{:S(2)}, u32[]{:S(2)}) collective-permute-start(bf16[2048,512]{1,0:T(8,128)(2,1)} %get-tuple-element.140.refs_5_.refs_4_.refs_3_), channel_id=1, source_target_pairs={{0,1},{1,0},{2,3},{3,2},{4,5},{5,4},{6,7},{7,6},{8,9},{9,8},{10,11... | collective-permute-start | bytes 6291464 | tf_op jit(solution)/shard_map/ppermute | solution.py:40
  15.1 38.9 %all-to-all-start = ((bf16[8,128,1024]{2,1,0:T(8,128)(2,1)}), bf16[8,128,1024]{2,1,0:T(8,128)(2,1)}, u32[]{:S(2)}, u32[]{:S(2)}) async-start(bf16[8,128,1024]{2,1,0:T(8,128)(2,1)} %shard_map.76), calls=%async_computation | async-start | bytes 4194304 | tf_op jit(solution)/shard_map/all_to_all | solution.py:315
  30.6 1.0 copy-start.5
  31.5 41.6 %collective-permute-start.3 = (bf16[128,4096]{1,0:T(8,128)(2,1)}, bf16[128,4096]{1,0:T(8,128)(2,1)S(1)}, u32[]{:S(2)}, u32[]{:S(2)}) collective-permute-start(bf16[128,4096]{1,0:T(8,128)(2,1)} %collective-permute-done.refs_3_), channel_id=1, source_target_pairs={{0,2},{1,3},{2,4},{3,5},{4,6},{5,7},{6,0},{7,1},{8,10},{9,11},{10,... | collective-permute-start | bytes 3145736 | tf_op jit(solution)/shard_map/ppermute | solution.py:40
  36.0 39.0 %collective-permute-start.5 = (bf16[128,4096]{1,0:T(8,128)(2,1)}, bf16[128,4096]{1,0:T(8,128)(2,1)}, u32[]{:S(2)}, u32[]{:S(2)}) collective-permute-start(bf16[128,4096]{1,0:T(8,128)(2,1)} %copy-done.5), channel_id=1, source_target_pairs={{0,8},{1,9},{2,10},{3,11},{4,12},{5,13},{6,14},{7,15},{8,0},{9,1},... | collective-permute-start | bytes 3145736 | tf_op jit(solution)/shard_map/ppermute | solution.py:40
  37.5 37.5 %collective-permute-start.4 = (bf16[128,4096]{1,0:T(8,128)(2,1)}, bf16[128,4096]{1,0:T(8,128)(2,1)}, u32[]{:S(2)}, u32[]{:S(2)}) collective-permute-start(bf16[128,4096]{1,0:T(8,128)(2,1)} %copy-done.5), channel_id=1, source_target_pairs={{0,6},{1,7},{2,0},{3,1},{4,2},{5,3},{6,4},{7,5},{8,14},{9,15},{10,... | collective-permute-start | bytes 3145736 | tf_op jit(solution)/shard_map/ppermute | solution.py:40
  73.1 5.1 %copy-start.2 = (bf16[128,4096]{1,0:T(8,128)(2,1)}, bf16[128,4096]{1,0:T(8,128)(2,1)S(1)}, u32[]{:S(2)}) copy-start(bf16[128,4096]{1,0:T(8,128)(2,1)S(1)} %collective-permute-done.3.refs_2_) | copy-start | bytes 3145732
  75.0 18.0 %collective-permute-start.10 = (bf16[512,4608]{1,0:T(8,128)(2,1)}, bf16[512,4608]{1,0:T(8,128)(2,1)}, u32[]{:S(2)}, u32[]{:S(2)}) collective-permute-start(bf16[512,4608]{1,0:T(8,128)(2,1)} %get-tuple-element.76.refs_0_), channel_id=1, source_target_pairs={{0,1},{1,0},{2,3},{3,2},{4,5},{5,4},{6,7},{7,6},{8,9},{9,8},{10,11... | collective-permute-start | bytes 14155784 | tf_op jit(solution)/shard_map/ppermute | solution.py:40
  76.1 16.2 %collective-permute-start.9 = (bf16[64,4096]{1,0:T(8,128)(2,1)S(1)}, bf16[64,4096]{1,0:T(8,128)(2,1)S(1)}, u32[]{:S(2)}, u32[]{:S(2)}) collective-permute-start(bf16[64,4096]{1,0:T(8,128)(2,1)S(1)} %slice.31), channel_id=1, source_target_pairs={{0,6},{1,7},{2,0},{3,1},{4,2},{5,3},{6,4},{7,5},{8,14},{9,15},{10,... | collective-permute-start | bytes 1572872 | tf_op jit(solution)/shard_map/ppermute | solution.py:40
  77.7 15.3 %collective-permute-start.8 = (bf16[64,4096]{1,0:T(8,128)(2,1)S(1)}, bf16[64,4096]{1,0:T(8,128)(2,1)S(1)}, u32[]{:S(2)}, u32[]{:S(2)}) collective-permute-start(bf16[64,4096]{1,0:T(8,128)(2,1)S(1)} %slice.30), channel_id=1, source_target_pairs={{0,2},{1,3},{2,4},{3,5},{4,6},{5,7},{6,0},{7,1},{8,10},{9,11},{10,... | collective-permute-start | bytes 1572872 | tf_op jit(solution)/shard_map/ppermute | solution.py:40
  92.3 0.8 copy-start.11
  93.0 0.8 copy-start.12
  93.7 17.8 %collective-permute-start.13 = (bf16[384,4608]{1,0:T(8,128)(2,1)}, bf16[384,4608]{1,0:T(8,128)(2,1)S(1)}, u32[]{:S(2)}, u32[]{:S(2)}) collective-permute-start(bf16[384,4608]{1,0:T(8,128)(2,1)} %get-tuple-element.84.refs_1_), channel_id=1, source_target_pairs={{0,1},{1,0},{2,3},{3,2},{4,5},{5,4},{6,7},{7,6},{8,9},{9,8},{10,11... | collective-permute-start | bytes 10616840 | tf_op jit(solution)/shard_map/ppermute | solution.py:40
  93.7 14.5 %collective-permute-start.11 = (bf16[64,4096]{1,0:T(8,128)(2,1)}, bf16[64,4096]{1,0:T(8,128)(2,1)S(1)}, u32[]{:S(2)}, u32[]{:S(2)}) collective-permute-start(bf16[64,4096]{1,0:T(8,128)(2,1)} %get-tuple-element.85), channel_id=1, source_target_pairs={{0,6},{1,7},{2,0},{3,1},{4,2},{5,3},{6,4},{7,5},{8,14},{9,15},{10,... | collective-permute-start | bytes 1572872 | tf_op jit(solution)/shard_map/ppermute | solution.py:40
  96.0 15.6 %collective-permute-start.12 = (bf16[64,4096]{1,0:T(8,128)(2,1)}, bf16[64,4096]{1,0:T(8,128)(2,1)}, u32[]{:S(2)}, u32[]{:S(2)}) collective-permute-start(bf16[64,4096]{1,0:T(8,128)(2,1)} %get-tuple-element.86), channel_id=1, source_target_pairs={{0,2},{1,3},{2,4},{3,5},{4,6},{5,7},{6,0},{7,1},{8,10},{9,11},{10,... | collective-permute-start | bytes 1572872 | tf_op jit(solution)/shard_map/ppermute | solution.py:40
  108.3 7.2 %copy-start.13 = (bf16[64,4096]{1,0:T(8,128)(2,1)}, bf16[64,4096]{1,0:T(8,128)(2,1)S(1)}, u32[]{:S(2)}) copy-start(bf16[64,4096]{1,0:T(8,128)(2,1)S(1)} %collective-permute-done.11) | copy-start | bytes 1572868
  111.6 3.9 %copy-start.1 = (bf16[384,4608]{1,0:T(8,128)(2,1)}, bf16[384,4608]{1,0:T(8,128)(2,1)S(1)}, u32[]{:S(2)}) copy-start(bf16[384,4608]{1,0:T(8,128)(2,1)S(1)} %collective-permute-done.13.refs_7_) | copy-start | bytes 10616836
  111.6 3.9 %collective-permute-start.14 = (bf16[128,4608]{1,0:T(8,128)(2,1)}, bf16[128,4608]{1,0:T(8,128)(2,1)}, u32[]{:S(2)}, u32[]{:S(2)}) collective-permute-start(bf16[128,4608]{1,0:T(8,128)(2,1)} %get-tuple-element.92.refs_2_), channel_id=1, source_target_pairs={{0,1},{1,0},{2,3},{3,2},{4,5},{5,4},{6,7},{7,6},{8,9},{9,8},{10,11... | collective-permute-start | bytes 3538952 | tf_op jit(solution)/shard_map/ppermute | solution.py:40
  111.6 14.8 %collective-permute-start.15 = (bf16[64,4096]{1,0:T(8,128)(2,1)}, bf16[64,4096]{1,0:T(8,128)(2,1)}, u32[]{:S(2)}, u32[]{:S(2)}) collective-permute-start(bf16[64,4096]{1,0:T(8,128)(2,1)} %get-tuple-element.98), channel_id=1, source_target_pairs={{0,6},{1,7},{2,0},{3,1},{4,2},{5,3},{6,4},{7,5},{8,14},{9,15},{10,... | collective-permute-start | bytes 1572872 | tf_op jit(solution)/shard_map/ppermute | solution.py:40
  112.1 15.3 %collective-permute-start.16 = (bf16[64,4096]{1,0:T(8,128)(2,1)}, bf16[64,4096]{1,0:T(8,128)(2,1)}, u32[]{:S(2)}, u32[]{:S(2)}) collective-permute-start(bf16[64,4096]{1,0:T(8,128)(2,1)} %get-tuple-element.99), channel_id=1, source_target_pairs={{0,2},{1,3},{2,4},{3,5},{4,6},{5,7},{6,0},{7,1},{8,10},{9,11},{10,... | collective-permute-start | bytes 1572872 | tf_op jit(solution)/shard_map/ppermute | solution.py:40
  113.9 32.1 %collective-permute-start.17 = (bf16[128,4096]{1,0:T(8,128)(2,1)}, bf16[128,4096]{1,0:T(8,128)(2,1)}, u32[]{:S(2)}, u32[]{:S(2)}) collective-permute-start(bf16[128,4096]{1,0:T(8,128)(2,1)} %get-tuple-element.108), channel_id=1, source_target_pairs={{0,8},{1,9},{2,10},{3,11},{4,12},{5,13},{6,14},{7,15},{8,0},{9,1},... | collective-permute-start | bytes 3145736 | tf_op jit(solution)/shard_map/ppermute | solution.py:40
  115.5 17.1 %copy-start.8 = (bf16[64,4096]{1,0:T(8,128)(2,1)S(1)}, bf16[64,4096]{1,0:T(8,128)(2,1)}, u32[]{:S(2)}) copy-start(bf16[64,4096]{1,0:T(8,128)(2,1)} %get-tuple-element.113) | copy-start | bytes 1572868
  127.4 18.6 %collective-permute-start.18 = (bf16[512,512]{1,0:T(8,128)(2,1)}, bf16[512,512]{1,0:T(8,128)(2,1)S(1)}, u32[]{:S(2)}, u32[]{:S(2)}) collective-permute-start(bf16[512,512]{1,0:T(8,128)(2,1)} %get-tuple-element.109), channel_id=1, source_target_pairs={{0,16},{16,32},{32,48},{48,0},{64,80},{80,96},{96,112},{112,64},{1... | collective-permute-start | bytes 1572872 | tf_op jit(solution)/shard_map/ppermute | solution.py:44
  129.0 17.0 %collective-permute-start.19 = (bf16[512,512]{1,0:T(8,128)(2,1)}, bf16[512,512]{1,0:T(8,128)(2,1)S(1)}, u32[]{:S(2)}, u32[]{:S(2)}) collective-permute-start(bf16[512,512]{1,0:T(8,128)(2,1)} %get-tuple-element.110), channel_id=1, source_target_pairs={{0,48},{16,0},{32,16},{48,32},{64,112},{80,64},{96,80},{112,96},{1... | collective-permute-start | bytes 1572872 | tf_op jit(solution)/shard_map/ppermute | solution.py:44
  132.0 14.1 %collective-permute-start.20 = (bf16[64,4096]{1,0:T(8,128)(2,1)S(1)}, bf16[64,4096]{1,0:T(8,128)(2,1)S(1)}, u32[]{:S(2)}, u32[]{:S(2)}) collective-permute-start(bf16[64,4096]{1,0:T(8,128)(2,1)S(1)} %add_convert_fusion.8), channel_id=1, source_target_pairs={{0,6},{1,7},{2,0},{3,1},{4,2},{5,3},{6,4},{7,5},{8,14},{9,15},{10,... | collective-permute-start | bytes 1572872 | tf_op jit(solution)/shard_map/ppermute | solution.py:40
  133.7 13.8 %copy-start.10 = (bf16[512,512]{1,0:T(8,128)(2,1)S(1)}, bf16[512,512]{1,0:T(8,128)(2,1)}, u32[]{:S(2)}) copy-start(bf16[512,512]{1,0:T(8,128)(2,1)} %get-tuple-element.107) | copy-start | bytes 1572868
  133.7 13.8 %collective-permute-start.21 = (bf16[64,4096]{1,0:T(8,128)(2,1)S(1)}, bf16[64,4096]{1,0:T(8,128)(2,1)S(1)}, u32[]{:S(2)}, u32[]{:S(2)}) collective-permute-start(bf16[64,4096]{1,0:T(8,128)(2,1)S(1)} %add_convert_fusion.7), channel_id=1, source_target_pairs={{0,2},{1,3},{2,4},{3,5},{4,6},{5,7},{6,0},{7,1},{8,10},{9,11},{10,... | collective-permute-start | bytes 1572872 | tf_op jit(solution)/shard_map/ppermute | solution.py:40
  146.0 6.2 %copy-start.7 = (bf16[128,4096]{1,0:T(8,128)(2,1)S(1)}, bf16[128,4096]{1,0:T(8,128)(2,1)}, u32[]{:S(2)}) copy-start(bf16[128,4096]{1,0:T(8,128)(2,1)} %get-tuple-element.126) | copy-start | bytes 3145732
  147.7 12.9 %collective-permute-start.22 = (bf16[512,512]{1,0:T(8,128)(2,1)S(1)}, bf16[512,512]{1,0:T(8,128)(2,1)S(1)}, u32[]{:S(2)}, u32[]{:S(2)}) collective-permute-start(bf16[512,512]{1,0:T(8,128)(2,1)S(1)} %add_convert_fusion.6), channel_id=1, source_target_pairs={{0,16},{16,32},{32,48},{48,0},{64,80},{80,96},{96,112},{112,64},{1... | collective-permute-start | bytes 1572872 | tf_op jit(solution)/shard_map/ppermute | solution.py:44
  148.0 12.6 %collective-permute-start.23 = (bf16[512,512]{1,0:T(8,128)(2,1)}, bf16[512,512]{1,0:T(8,128)(2,1)S(1)}, u32[]{:S(2)}, u32[]{:S(2)}) collective-permute-start(bf16[512,512]{1,0:T(8,128)(2,1)} %get-tuple-element.119), channel_id=1, source_target_pairs={{0,48},{16,0},{32,16},{48,32},{64,112},{80,64},{96,80},{112,96},{1... | collective-permute-start | bytes 1572872 | tf_op jit(solution)/shard_map/ppermute | solution.py:44
  152.2 1.8 copy-start.6
  152.3 1.8 copy-start.14
  153.7 3.9 %copy-start.4 = (bf16[128,4096]{1,0:T(8,128)(2,1)S(1)}, bf16[128,4096]{1,0:T(8,128)(2,1)}, u32[]{:S(2)}) copy-start(bf16[128,4096]{1,0:T(8,128)(2,1)} %get-tuple-element.128) | copy-start | bytes 3145732
  153.7 23.8 %collective-permute-start.25 = (bf16[128,4096]{1,0:T(8,128)(2,1)S(1)}, bf16[128,4096]{1,0:T(8,128)(2,1)S(1)}, u32[]{:S(2)}, u32[]{:S(2)}) collective-permute-start(bf16[128,4096]{1,0:T(8,128)(2,1)S(1)} %add_convert_fusion.2), channel_id=1, source_target_pairs={{0,2},{1,3},{2,4},{3,5},{4,6},{5,7},{6,0},{7,1},{8,10},{9,11},{10,... | collective-permute-start | bytes 3145736 | tf_op jit(solution)/shard_map/ppermute | solution.py:40
  154.3 6.3 %copy-start.9 = (bf16[512,512]{1,0:T(8,128)(2,1)S(1)}, bf16[512,512]{1,0:T(8,128)(2,1)}, u32[]{:S(2)}) copy-start(bf16[512,512]{1,0:T(8,128)(2,1)} %get-tuple-element.132) | copy-start | bytes 1572868
  154.3 22.8 %collective-permute-start.24 = (bf16[128,4096]{1,0:T(8,128)(2,1)S(1)}, bf16[128,4096]{1,0:T(8,128)(2,1)S(1)}, u32[]{:S(2)}, u32[]{:S(2)}) collective-permute-start(bf16[128,4096]{1,0:T(8,128)(2,1)S(1)} %add_convert_fusion.3), channel_id=1, source_target_pairs={{0,6},{1,7},{2,0},{3,1},{4,2},{5,3},{6,4},{7,5},{8,14},{9,15},{10,... | collective-permute-start | bytes 3145736 | tf_op jit(solution)/shard_map/ppermute | solution.py:40
  157.6 6.3 %copy-start.16 = (bf16[512,512]{1,0:T(8,128)(2,1)S(1)}, bf16[512,512]{1,0:T(8,128)(2,1)}, u32[]{:S(2)}) copy-start(bf16[512,512]{1,0:T(8,128)(2,1)} %get-tuple-element.135) | copy-start | bytes 1572868
  157.8 19.3 %copy-start.17 = (bf16[512,512]{1,0:T(8,128)(2,1)S(1)}, bf16[512,512]{1,0:T(8,128)(2,1)}, u32[]{:S(2)}) copy-start(bf16[512,512]{1,0:T(8,128)(2,1)} %get-tuple-element.134) | copy-start | bytes 1572868
  157.8 26.2 %copy-start.3 = (bf16[128,4096]{1,0:T(8,128)(2,1)S(1)}, bf16[128,4096]{1,0:T(8,128)(2,1)}, u32[]{:S(2)}) copy-start(bf16[128,4096]{1,0:T(8,128)(2,1)} %get-tuple-element.106) | copy-start | bytes 3145732
  157.9 26.2 %collective-permute-start.26 = (bf16[128,4096]{1,0:T(8,128)(2,1)S(1)}, bf16[128,4096]{1,0:T(8,128)(2,1)S(1)}, u32[]{:S(2)}, u32[]{:S(2)}) collective-permute-start(bf16[128,4096]{1,0:T(8,128)(2,1)S(1)} %add_convert_fusion.1), channel_id=1, source_target_pairs={{0,8},{1,9},{2,10},{3,11},{4,12},{5,13},{6,14},{7,15},{8,0},{9,1},... | collective-permute-start | bytes 3145736 | tf_op jit(solution)/shard_map/ppermute | solution.py:40
  160.7 25.0 %collective-permute-start.27 = (bf16[512,512]{1,0:T(8,128)(2,1)S(1)}, bf16[512,512]{1,0:T(8,128)(2,1)S(1)}, u32[]{:S(2)}, u32[]{:S(2)}) collective-permute-start(bf16[512,512]{1,0:T(8,128)(2,1)S(1)} %add_convert_fusion.5), channel_id=1, source_target_pairs={{0,48},{16,0},{32,16},{48,32},{64,112},{80,64},{96,80},{112,96},{1... | collective-permute-start | bytes 1572872 | tf_op jit(solution)/shard_map/ppermute | solution.py:44
  164.1 28.7 %collective-permute-start.29 = (bf16[512,512]{1,0:T(8,128)(2,1)S(1)}, bf16[512,512]{1,0:T(8,128)(2,1)S(1)}, u32[]{:S(2)}, u32[]{:S(2)}) collective-permute-start(bf16[512,512]{1,0:T(8,128)(2,1)S(1)} %add_convert_fusion.4), channel_id=1, source_target_pairs={{0,64},{16,80},{32,96},{48,112},{64,0},{80,16},{96,32},{112,48},{1... | collective-permute-start | bytes 1572872 | tf_op jit(solution)/shard_map/ppermute | solution.py:44
  177.1 15.8 %collective-permute-start.28 = (bf16[512,512]{1,0:T(8,128)(2,1)S(1)}, bf16[512,512]{1,0:T(8,128)(2,1)S(1)}, u32[]{:S(2)}, u32[]{:S(2)}) collective-permute-start(bf16[512,512]{1,0:T(8,128)(2,1)S(1)} %copy-done.17), channel_id=1, source_target_pairs={{0,16},{16,32},{32,48},{48,0},{64,80},{80,96},{96,112},{112,64},{1... | collective-permute-start | bytes 1572872 | tf_op jit(solution)/shard_map/ppermute | solution.py:44
  184.0 8.8 %copy-start.15 = (bf16[512,512]{1,0:T(8,128)(2,1)S(1)}, bf16[512,512]{1,0:T(8,128)(2,1)}, u32[]{:S(2)}) copy-start(bf16[512,512]{1,0:T(8,128)(2,1)} %get-tuple-element.131) | copy-start | bytes 1572868
